TPU v7x, 128 devices: a whole 4x4x4 slice. The times are simulated.
128 devices in a mesh: row: 8 (over x, core), col: 16 (over y, z).
Axes of the slice: x: 4, y: 4, z: 4, core: 2. Of those that a mesh axis runs over, the one named last changes fastest.
Arguments:
- blocks_a: bfloat16 [64, 256, 138, 138], P('row', 'col'), may hold values from -6 to 6
- pattern_a: int32 [64, 256], P('row', 'col'), may hold values 0 or 1
- blocks_b: bfloat16 [256, 16, 138, 138], P('col'), may hold values from -0.0625 to 0.0625
- filter_mask: int32 [64, 16], P('row', 'col'), may hold values 0 or 1
- task_brick: int32 [64, 16], P('row', 'col'), may hold values from 0 to 127
- basis_rows: bfloat16 [64, 138, 16384], P('row'), may hold values from -0.5 to 0.5
- basis_cols: bfloat16 [16, 138, 16384], P('col'), may hold values from -0.5 to 0.5
- kernel: float32 [1024, 2048], P(('row', 'col')), may hold values from 0.1 to 10
Outputs:
- density: bfloat16 [64, 16, 138, 138], P('row', 'col')
- potential: float32 [1024, 2048], P('row', 'col')
Inputs may be any that keep to these rules, and one draw needn't show every extreme that they name: `pattern_a`: 1 marks a block that is kept. `filter_mask`: 1 marks a product block that is kept.
All inputs are finite; a program needn't handle non-finite values.
Results may differ from a plain program's by a relative error of at most 0.0028.
Values may be sent and summed in bfloat16 or wider, within the bound.
No kernel may reach another device: no remote copies, remote signals or barrier semaphores. Data moves between devices by JAX's collectives and lax.ppermute only.
A program may use at most 576 MiB of HBM per device.

v0:
```python
import functools
import math

import jax
import jax.numpy as jnp
import numpy as np
from jax import lax
from jax.experimental import pallas as pl
from jax.experimental.pallas import tpu as pltpu
from jax.sharding import PartitionSpec as P

BS = 138
MIB = 1 << 20
HIGH = lax.Precision.HIGHEST
F32 = jnp.float32
BF16 = jnp.bfloat16
I16 = jnp.int16
WIDE = 2304
SPAN = 1152
ROWS = (672, 432)
CUT = (0, 672)
TOP = (336, 224)
FOLD = (96, 64)
STEP = (28, 18)
POINTS = 2048


def in_hbm(array):
    return pltpu.with_memory_space_constraint(array, pltpu.HBM)


def widen(tail):
    return jnp.concatenate([tail.astype(F32), jnp.zeros(tail.shape[:-1] + (128 - tail.shape[-1],), F32)], axis=-1)


def place_tails(tails, out, rows):
    lane = lax.broadcasted_iota(jnp.int32, (16, 128), 1) // 16
    for half in range(2):
        rest = jnp.zeros((16, 128), F32)
        for n in range(8):
            tail = tails[half * 8 + n]
            rest = jnp.where(lane == n, pltpu.roll(tail, 16 * n, 1) if n else tail, rest)
        out(half, rest.astype(BF16))


def pack_left_kernel(pairs, mask, blocks, after, out):
    def step(p, carry):
        pair = jnp.transpose(blocks[:, pl.ds(2 * p, 2)], (1, 0, 2, 3)).reshape(16, 16, BS)
        wide = jnp.swapaxes(pair, 0, 1)
        rows = pl.ds(pl.multiple_of(16 * p, 16), 16)
        tails = []
        for k in range(16):
            at = SPAN * (k // 8) + 128 * (k % 8)
            out[rows, at : at + 128] = wide[k, :, :128] * mask[k]
            tails.append(widen(wide[k, :, 128:] * mask[k, :, : BS - 128]))

        def put(half, value):
            out[rows, SPAN * half + 1024 : SPAN * half + 1152] = value

        place_tails(tails, put, rows)
        return carry

    lax.fori_loop(0, pairs, step, 0)


def pack_left(half, mask, blocks, after):
    count = STEP[half]
    return pl.pallas_call(
        functools.partial(pack_left_kernel, count // 2),
        grid=(ROWS[half] // 8 // count,),
        in_specs=[
            pl.BlockSpec((16, 16, 128), lambda g: (0, 0, 0)),
            pl.BlockSpec(
                (pl.Element(8), pl.Element(count), pl.Element(16), pl.Element(BS)),
                lambda g: (0, CUT[half] // 8 + count * g, 0, 0),
            ),
            pl.BlockSpec(memory_space=pl.ANY),
        ],
        out_specs=pl.BlockSpec((count * 8, WIDE), lambda g: (g, 0)),
        out_shape=pltpu.VMEM((ROWS[half], WIDE), BF16),
        compiler_params=pltpu.CompilerParams(vmem_limit_bytes=32 * MIB),
        cost_estimate=pl.CostEstimate(flops=1000, bytes_accessed=1000, transcendentals=0),
        name="pack_left",
    )(mask, in_hbm(blocks), after)


def pack_right_kernel(blocks, *others):
    near, rest = others[-2:]
    base = pl.program_id(0) % 4 * 2

    def step(n, carry):
        k = base + n
        for c in range(0, 144, 16):
            if c < 128:
                rows = pl.ds(pl.multiple_of(128 * k + c, 16), 16)
                square = blocks[n, c : c + 16]
            else:
                rows = pl.ds(pl.multiple_of(1024 + 16 * k, 16), 16)
                square = jnp.concatenate([blocks[n, 128:BS], jnp.zeros((144 - BS, 16, BS), BF16)], axis=0)
            turned = jnp.swapaxes(square, 0, 1)
            near[:, rows, :] = turned[:, :, :128]

            def put(half, value, rows=rows):
                rest[rows, 128 * half : 128 * half + 128] = value

            place_tails([widen(turned[j, :, 128:]) for j in range(16)], put, rows)
        return carry

    lax.fori_loop(0, 2, step, 0)


def pack_right(blocks, before):
    return pl.pallas_call(
        pack_right_kernel,
        grid=(8,),
        in_specs=[pl.BlockSpec((2, BS, 16, BS), lambda g: (g, 0, 0, 0))]
        + [pl.BlockSpec(memory_space=pl.ANY)] * len(before),
        out_specs=[
            pl.BlockSpec((16, SPAN, 128), lambda g: (0, g // 4, 0)),
            pl.BlockSpec((SPAN, 256), lambda g: (g // 4, 0)),
        ],
        out_shape=[
            pltpu.VMEM((16, WIDE, 128), BF16),
            pltpu.VMEM((WIDE, 256), BF16),
        ],
        compiler_params=pltpu.CompilerParams(vmem_limit_bytes=24 * MIB),
        cost_estimate=pl.CostEstimate(flops=1000, bytes_accessed=1000, transcendentals=0),
        name="pack_right",
    )(in_hbm(blocks), *before)


def tails_kernel(half, left, rest, swap, after, out):
    right = rest[...]
    if half == 1:
        right = jnp.dot(right, swap[...], preferred_element_type=F32).astype(BF16)
    out[...] = jnp.dot(left[...], right, preferred_element_type=F32)


def product_tails(half, left, rest, after):
    lane = np.arange(256)
    swap = np.zeros((256, 256), np.float32)
    swap[lane, lane // 16 % 4 * 64 + lane // 64 * 16 + lane % 16] = 1.0
    vmem = pl.BlockSpec(memory_space=pltpu.VMEM)
    return pl.pallas_call(
        functools.partial(tails_kernel, half),
        in_specs=[vmem] * 3 + [pl.BlockSpec(memory_space=pl.ANY)],
        out_specs=vmem,
        out_shape=jax.ShapeDtypeStruct((ROWS[half], 256), F32),
        compiler_params=pltpu.CompilerParams(vmem_limit_bytes=12 * MIB),
        cost_estimate=pl.CostEstimate(flops=1000, bytes_accessed=1000, transcendentals=0),
        name="product_tails",
    )(left, rest, jnp.asarray(swap, BF16), after)


def padded(value, rows):
    if value.shape[0] == rows:
        return value
    return jnp.concatenate([value, jnp.zeros((rows - value.shape[0], 128), F32)], axis=0)


def lanes(rows):
    return lax.broadcasted_iota(jnp.int32, (rows, 128), 1)


def scale_of(most):
    power = jnp.floor(jnp.log2(jnp.maximum(jnp.full((1, 128), most, F32), 1e-30))) + 1.0
    return power, 32000.0 * jnp.exp2(-power)


def gain_of(coded):
    power = jnp.max(jnp.where(lanes(16) % 16 == 15, coded[0:16], -1000.0))
    return jnp.exp2(jnp.full((1, 128), power, F32)) * (1.0 / 32000.0)


def code(value, gain):
    return jnp.round(value * gain).astype(jnp.int32).astype(I16)


def code_tail(value, gain, power):
    coded = jnp.where(lanes(value.shape[0]) % 16 == 15, jnp.broadcast_to(power, value.shape), jnp.round(value * gain))
    return coded.astype(jnp.int32).astype(I16)


def plain(value):
    return value.astype(jnp.int32).astype(F32)


def product_kernel(half, d, spot, left, near, tails, after, out, held):
    rows = ROWS[half]
    coded = d != 0
    group = (spot[half] + d) % 4
    which = [4 * group + n if half == 0 else 4 * n + group for n in range(4)]
    for pair in range(2):
        both = jnp.dot(
            left[...],
            jnp.concatenate([near[which[2 * pair]], near[which[2 * pair + 1]]], axis=1),
            preferred_element_type=F32,
        )
        if coded:
            held[2 * pair] = both[:, :128]
            held[2 * pair + 1] = both[:, 128:]
        else:
            out[2 * pair * rows : (2 * pair + 1) * rows, :] = both[:, :128]
            out[(2 * pair + 1) * rows : (2 * pair + 2) * rows, :] = both[:, 128:]
    tail = jnp.where(group >= 2, tails[:, 128:], tails[:, :128])
    top = TOP[half]
    high, low = tail[:top], padded(tail[top:], top)
    odd = group % 2 == 1
    folded = jnp.where(
        lanes(top) < 64,
        jnp.where(odd, pltpu.roll(high, 64, 1), high),
        jnp.where(odd, low, pltpu.roll(low, 64, 1)),
    )
    if coded:
        power, gain = scale_of(jnp.maximum(jnp.max(jnp.abs(held[...])), jnp.max(jnp.abs(folded))))
        for n in range(4):
            out[n * rows : (n + 1) * rows, :] = code(held[n], gain)
        out[4 * rows : 4 * rows + TOP[half], :] = code_tail(folded, gain, power)
    else:
        out[4 * rows : 4 * rows + TOP[half], :] = folded


def product_group(half, d, spot, left, near, tails, after):
    rows = ROWS[half]
    coded = d != 0
    vmem = pl.BlockSpec(memory_space=pltpu.VMEM)
    return pl.pallas_call(
        functools.partial(product_kernel, half, d),
        in_specs=[pl.BlockSpec(memory_space=pltpu.SMEM)] + [vmem] * 3 + [pl.BlockSpec(memory_space=pl.ANY)],
        out_specs=vmem,
        out_shape=jax.ShapeDtypeStruct((4 * rows + TOP[half], 128), I16 if coded else F32),
        scratch_shapes=[pltpu.VMEM((4, rows, 128), F32)],
        compiler_params=pltpu.CompilerParams(vmem_limit_bytes=10 * MIB),
        cost_estimate=pl.CostEstimate(flops=1000, bytes_accessed=1000, transcendentals=0),
        name="product_coded" if coded else "product_own",
    )(spot, left, near, tails, after)


def merge_kernel(half, place, own, in1, in2, in3, after, mine, out1, out2, out3, held):
    rows, top, size = ROWS[half], TOP[half], FOLD[half]
    parts = (in1, in2, in3)
    tails = [plain(p[4 * rows : 4 * rows + top, :]) for p in parts]
    gains = [gain_of(t) for t in tails]
    for n in range(4):
        here = slice(n * rows, (n + 1) * rows)
        total = own[here, :]
        for p, g in zip(parts, gains):
            total = total + plain(p[here, :]) * g
        held[n] = total
    folded = own[4 * rows : 4 * rows + top, :]
    for t, g in zip(tails, gains):
        folded = folded + t * g
    pieces = [padded(folded[q * size : min(top, (q + 1) * size)], size) for q in range(4)]
    slot = lanes(size) // 16 % 4
    for s in range(4):

        @pl.when(place[1 - half] == s)
        def _(s=s):
            for d, out in enumerate((mine, out1, out2, out3)):
                here = (s + d) % 4
                tail = jnp.zeros((size, 128), F32)
                for q in range(4):
                    tail = jnp.where(slot == q, pltpu.roll(pieces[q], 16 * ((q - here) % 8), 1) if (q - here) % 8 else pieces[q], tail)
                main = held[here]
                if d == 0:
                    out[0:rows, :] = main
                    out[rows : rows + size, :] = tail
                else:
                    tail = jnp.where(lanes(size) % 16 < 10, tail, 0.0)
                    power, gain = scale_of(jnp.maximum(jnp.max(jnp.abs(main)), jnp.max(jnp.abs(tail))))
                    out[0:rows, :] = code(main, gain)
                    out[rows : rows + size, :] = code_tail(tail, gain, power)


def merge(half, place, own, parts, after):
    vmem = pl.BlockSpec(memory_space=pltpu.VMEM)
    return pl.pallas_call(
        functools.partial(merge_kernel, half),
        in_specs=[pl.BlockSpec(memory_space=pltpu.SMEM)] + [vmem] * 4 + [pl.BlockSpec(memory_space=pl.ANY)],
        out_specs=[vmem] * 4,
        out_shape=[jax.ShapeDtypeStruct((ROWS[half] + FOLD[half], 128), t) for t in (F32, I16, I16, I16)],
        scratch_shapes=[pltpu.VMEM((4, ROWS[half], 128), F32)],
        compiler_params=pltpu.CompilerParams(vmem_limit_bytes=12 * MIB),
        cost_estimate=pl.CostEstimate(flops=1000, bytes_accessed=1000, transcendentals=0),
        name="merge",
    )(place, own, *parts, after)


def turn(dy, dz):
    return [(4 * y + z, (y + dy) % 4 * 4 + (z + dz) % 4) for y in range(4) for z in range(4)]


def send(array, axis, d):
    return lax.ppermute(array, "col", turn(d, 0) if axis == 0 else turn(0, d))


def exchange_products(blocks_a, pattern, blocks_b, before):
    place = lax.axis_index("col").astype(jnp.int32)
    spot = jnp.stack([place // 4, place % 4])
    mask = jnp.broadcast_to(jnp.tile(pattern.T, (1, 2))[:, :, None], (16, 16, 128)).astype(BF16)
    blocks_a = jnp.transpose(blocks_a, (0, 2, 1, 3))
    near, rest = pack_right(jnp.transpose(blocks_b, (0, 2, 1, 3)), [mask, spot] + before)
    after = near
    parts, owns = ([], []), []
    lefts = []
    for half in range(2):
        left = pack_left(half, mask, blocks_a, after)
        tails = product_tails(half, left, rest, after)
        lefts.append((left, near, tails))
        after = tails
        for d in (1, 2, 3):
            last = product_group(half, d, spot, *lefts[half], after)
            parts[half].append(send(last, half, d))
        after = last
    for half in range(2):
        after = product_group(half, 0, spot, *lefts[half], after)
        owns.append(after)

    def finish(half, after):
        mine, *outs = merge(half, spot, owns[half], parts[half], after)
        return mine, [send(outs[d - 1], 1 - half, d) for d in (2, 1, 3)]

    return finish, after


def collocate_kernel(half, keep, ids, own, in1, in2, in3, cols, rows, after, *rest):
    size = FOLD[half]
    if half == 0:
        density, out, stacked, right, held, held_cols, sems = rest
        before = None
    else:
        before, density, out, stacked, right, held, held_cols, sems = rest
    count = ROWS[half]
    tiles = 16384 // POINTS

    def copies(g):
        spot = pl.ds(pl.multiple_of(g * POINTS, POINTS), POINTS)
        return (
            pltpu.make_async_copy(cols.at[0, :, spot], held_cols.at[g], sems.at[0, g]),
            pltpu.make_async_copy(
                rows.at[pl.ds(CUT[half] // 8, count // 8), :, spot], held.at[g], sems.at[1, g]
            ),
        )

    for g in range(tiles):
        for copy in copies(g):
            copy.start()

    def decode_density():
        main, fold = own[0:count, :], own[count : count + size, :]
        for part in (in1, in2, in3):
            extra = plain(part[count : count + size, :])
            gain = gain_of(extra)
            main, fold = main + plain(part[0:count, :]) * gain, fold + extra * gain
        tails = []
        for base, total in ((0, TOP[half]), (4, count - TOP[half])):
            for q in range(4):
                piece = fold[0 : min(size, total - q * size)]
                shift = (128 - 16 * (q + base)) % 128
                tails.append(pltpu.roll(piece, shift, 1) if shift else piece)
        tail = jnp.where(lanes(count) < BS - 128, jnp.concatenate(tails, axis=0), 0.0)
        kept = keep[...][None]
        main = (main.reshape(count // 8, 8, 128) * kept).reshape(count, 128).astype(BF16)
        tail = (tail.reshape(count // 8, 8, 128) * kept).reshape(count, 128).astype(BF16)
        stacked[:, 0:128] = main
        stacked[:, 128:256] = tail
        density[:, :, 0:128] = main.reshape(count // 8, 8, 128)
        density[:, :, 128:BS] = tail.reshape(count // 8, 8, 128)[:, :, : BS - 128]
        right[128:256, :] = jnp.zeros((128, POINTS), BF16)

    decode_density()

    def step(g, carry):
        for copy in copies(g):
            copy.wait()
        right[0:BS, :] = held_cols[g]
        tile(g)
        return carry

    def tile(g):
        per = POINTS // 1024
        for t in range(POINTS // 256):
            here = slice(t * 256, (t + 1) * 256)
            inner = jnp.dot(stacked[...], right[:, here], preferred_element_type=F32).reshape(count // 8, 8, 256)
            total = jnp.sum(inner * held[g, :, :, here].astype(F32), axis=0)
            within = slice(t % 4 * 256, t % 4 * 256 + 256)
            if half == 1:
                total = total + before[per * g + t // 4, :, within]
            out[per * g + t // 4, :, within] = total
        if half == 1:
            for n in range(POINTS // 1024):
                out[per * g + n, :, 1024:1152] = ids[...]

    lax.fori_loop(0, tiles, step, 0)


def collocate(half, keep, ids, own, parts, basis_cols, basis_rows, before, after):
    count = ROWS[half]
    wide = 1152 if half else 1024
    vmem = pl.BlockSpec(memory_space=pltpu.VMEM)
    tiles = 16384 // POINTS
    return pl.pallas_call(
        functools.partial(collocate_kernel, half),
        in_specs=[vmem] * 6
        + [pl.BlockSpec(memory_space=pltpu.HBM)] * 2
        + [pl.BlockSpec(memory_space=pl.ANY)]
        + [vmem] * half,
        out_specs=[vmem] * 2,
        scratch_shapes=[
            pltpu.VMEM((count, 256), BF16),
            pltpu.VMEM((256, POINTS), BF16),
            pltpu.VMEM((tiles, count // 8, 8, POINTS), BF16),
            pltpu.VMEM((tiles, BS, POINTS), BF16),
            pltpu.SemaphoreType.DMA((2, tiles)),
        ],
        out_shape=[
            jax.ShapeDtypeStruct((count // 8, 8, BS), BF16),
            jax.ShapeDtypeStruct((16, 8, wide), F32),
        ],
        compiler_params=pltpu.CompilerParams(vmem_limit_bytes=(38, 28)[half] * MIB),
        cost_estimate=pl.CostEstimate(flops=1000, bytes_accessed=1000, transcendentals=0),
        name="collocate",
    )(keep, ids, own, *parts, in_hbm(basis_cols), in_hbm(basis_rows), after, *before)


def bricks_kernel(points, out):
    owners = jnp.sum(points[:, :, 1024:1152].reshape(128, 128), axis=0, keepdims=True).astype(jnp.int32)
    onehot = (owners == lax.broadcasted_iota(jnp.int32, (128, 128), 0)).astype(F32)
    held = points[:, :, 0:1024].reshape(128, 1024)
    out[...] = jnp.dot(onehot, held, precision=HIGH, preferred_element_type=F32)


def sum_bricks(points):
    return pl.pallas_call(
        bricks_kernel,
        out_shape=jax.ShapeDtypeStruct((128, 1024), F32),
        compiler_params=pltpu.CompilerParams(vmem_limit_bytes=8 * MIB),
        cost_estimate=pl.CostEstimate(flops=1000, bytes_accessed=1000, transcendentals=0),
        name="sum_bricks",
    )(points)


def tables():
    a = np.arange(16)
    outer = 2.0 * math.pi * (np.outer(a, a) % 16) / 16
    eye = np.eye(8)
    ck, sk = np.kron(eye, np.cos(outer)), np.kron(eye, np.sin(outer))
    b = np.arange(128)
    inner = 2.0 * math.pi * (np.outer(b, b) % 128) / 128
    c, s = np.cos(inner), np.sin(inner)
    twist = 2.0 * math.pi * np.outer(np.tile(a, 8), b) / 2048
    first = np.concatenate([ck, -sk], 0)
    second = np.block([[c, -s], [s, c]])
    third = np.block([[c, s], [-s, c]])
    last = np.concatenate([ck, -sk], 1) / 2048
    return [np.asarray(t, np.float32) for t in (first, second, third, last, np.cos(twist), np.sin(twist))]


def filter_kernel(own, in1, in2, in3, kern, first, second, third, last, tc, ts, out):
    def dot(p, q):
        return jnp.dot(p, q, precision=HIGH, preferred_element_type=F32)

    grid = (own[...] + in1[...]) + (in2[...] + in3[...])
    grid = jnp.concatenate([grid[:, y * 128 : y * 128 + 128] for y in range(8)], axis=0)
    section = dot(first[...], grid)
    re, im = section[:128], section[128:]
    c, s = tc[...], ts[...]
    spec = dot(jnp.concatenate([re * c + im * s, im * c - re * s], axis=1), second[...])
    k = kern[...]
    back = dot(spec * jnp.concatenate([k, k], axis=1), third[...])
    re, im = back[:, :128], back[:, 128:]
    turned = jnp.concatenate([re * c - im * s, im * c + re * s], axis=0)
    result = dot(last[...], turned)
    for y in range(8):
        out[:, y, :] = result[y * 16 : y * 16 + 16]


def filter_rows(pieces, kern):
    return pl.pallas_call(
        filter_kernel,
        out_shape=jax.ShapeDtypeStruct((16, 8, 128), F32),
        compiler_params=pltpu.CompilerParams(vmem_limit_bytes=8 * MIB),
        cost_estimate=pl.CostEstimate(flops=1000, bytes_accessed=1000, transcendentals=0),
        name="filter_rows",
    )(*pieces, kern, *tables())


def scatter_rows(partial):
    place = lax.axis_index("row")
    x, core = place // 2, place % 2
    halves = partial.reshape(4, 2, 16, 1024)
    away = lax.dynamic_index_in_dim(halves, 1 - core, 1, keepdims=False)
    mine = lax.dynamic_index_in_dim(halves, core, 1, keepdims=False)
    mine = mine + lax.ppermute(away, "row", [(r, r ^ 1) for r in range(8)])
    pieces = [lax.dynamic_index_in_dim(mine, x, 0, keepdims=False)]
    for d in (1, 2, 3):
        part = lax.dynamic_index_in_dim(mine, (x + d) % 4, 0, keepdims=False)
        pieces.append(lax.ppermute(part, "row", [(r, (r + 2 * d) % 8) for r in range(8)]))
    return pieces


def shards(blocks_a, pattern_a, blocks_b, filter_mask, task_brick, basis_rows, basis_cols, kernel):
    kern = jnp.transpose(kernel.reshape(8, 128, 16), (0, 2, 1)).reshape(128, 128)
    lane = jnp.arange(128, dtype=jnp.int32)
    owners = jnp.where(lane // 8 == lax.axis_index("col"), jnp.tile(task_brick.reshape(8), 16), 0)
    ids = jnp.concatenate([owners.astype(F32)[None], jnp.zeros((7, 128), F32)], axis=0)
    keep = jnp.broadcast_to(filter_mask.reshape(8, 1).astype(F32), (8, 128))
    by_point = jnp.transpose(basis_rows, (1, 0, 2))
    finish, after = exchange_products(blocks_a, pattern_a, blocks_b, [kern, ids, keep])
    densities, before, sums = [], [], []
    for half in range(2):
        sums.append(finish(half, after))
        after = sums[half][0]
    for half in range(2):
        own, parts = sums[half]
        density, after = collocate(half, keep, ids, own, parts, basis_cols, by_point, before, after)
        densities.append(density)
        before = [after]
    points = after
    points = lax.all_to_all(points, "col", split_axis=0, concat_axis=0, tiled=True)
    pieces = scatter_rows(sum_bricks(points))
    filtered = filter_rows(pieces, kern)
    potential = lax.all_to_all(filtered, "col", split_axis=0, concat_axis=0, tiled=True)
    density = jnp.transpose(jnp.concatenate(densities, axis=0), (1, 0, 2))
    return density[:, None], potential.reshape(128, 128)


def solution(mesh):
    return jax.shard_map(
        shards,
        mesh=mesh,
        in_specs=(
            P("row", "col", None, None),
            P("row", "col"),
            P("col", None, None, None),
            P("row", "col"),
            P("row", "col"),
            P("row", None, None),
            P("col", None, None),
            P(("row", "col"), None),
        ),
        out_specs=(P("row", "col", None, None), P("row", "col")),
        check_vma=False,
    )
```

profile of v0, /device:TPU:0, one launch (start us, length us, event | category | flops | bytes accessed | tf_op | source)
XLA Modules:
  0.0 143.2 jit_solution(18390435254963536057)
XLA Ops:
  4.3 12.5 %pack_right.1 = (bf16[16,2304,128]{2,1,0:T(8,128)(2,1)S(1)}, bf16[2304,256]{1,0:T(8,128)(2,1)S(1)}) custom-call(bf16[16,138,16,138]{3,2,1,0:T(8,128)(2,1)} %bitcast.40, bf16[16,16,128]{2,1,0:T(8,128)(2,1)S(1)} %broadcast_in_dim.21.others_0_.mask, s32[2]{0:T(128)S(1)} %pad_add_fusion.others_1_.spot.place, f32[128,128]{1,0:T(8,128)S(1)} %bitcast.34, ...), custom_call_target="tpu_custom_call" | custom-call | flops 1000 | bytes 1000 | tf_op jit(solution)/shard_map/pack_right/pallas_call | solution.py:113
  16.9 7.0 %pack_left.2.left = bf16[672,2304]{1,0:T(8,128)(2,1)S(1)} custom-call(bf16[16,16,128]{2,1,0:T(8,128)(2,1)S(1)} %broadcast_in_dim.21.others_0_.mask, bf16[8,138,16,138]{3,2,1,0:T(8,128)(2,1)} %bitcast.38, bf16[16,2304,128]{2,1,0:T(8,128)(2,1)S(1)} %get-tuple-element.16.after.near), custom_call_target="tpu_custom_call" | custom-call | flops 1000 | bytes 1000 | tf_op jit(solution)/shard_map/pack_left/pallas_call | solution.py:68
  24.9 2.8 %product_coded.9 = s16[3024,128]{1,0:T(8,128)(2,1)S(1)} custom-call(s32[2]{0:T(128)S(1)} %pad_add_fusion.others_1_.spot.place, bf16[672,2304]{1,0:T(8,128)(2,1)S(1)} %pack_left.2.left, bf16[16,2304,128]{2,1,0:T(8,128)(2,1)S(1)} %get-tuple-element.16.after.near, f32[672,256]{1,0:T(8,128)S(1)} %product_tails.2.tails.after, f32[672,256]{1,0:T(8,128)S(1)} %product_tails.2.tails.after), custom_call_target="tpu_custom_call" | custom-call | flops 1000 | bytes 1000 | tf_op jit(solution)/shard_map/product_coded/pallas_call | solution.py:227
  27.7 3.4 %collective-permute-start.1 = (s16[3024,128]{1,0:T(8,128)(2,1)S(1)}, s16[3024,128]{1,0:T(8,128)(2,1)S(1)}, u32[]{:S(2)}, u32[]{:S(2)}) collective-permute-start(s16[3024,128]{1,0:T(8,128)(2,1)S(1)} %product_coded.9), channel_id=1, source_target_pairs={{0,8},{1,9},{2,10},{3,11},{4,12},{5,13},{6,14},{7,15},{8,0},{9,1},... | collective-permute-start | bytes 2322440 | tf_op jit(solution)/shard_map/ppermute | solution.py:294
  31.0 2.8 %product_coded.8 = s16[3024,128]{1,0:T(8,128)(2,1)S(1)} custom-call(s32[2]{0:T(128)S(1)} %pad_add_fusion.others_1_.spot.place, bf16[672,2304]{1,0:T(8,128)(2,1)S(1)} %pack_left.2.left, bf16[16,2304,128]{2,1,0:T(8,128)(2,1)S(1)} %get-tuple-element.16.after.near, f32[672,256]{1,0:T(8,128)S(1)} %product_tails.2.tails.after, f32[672,256]{1,0:T(8,128)S(1)} %product_tails.2.tails.after), custom_call_target="tpu_custom_call" | custom-call | flops 1000 | bytes 1000 | tf_op jit(solution)/shard_map/product_coded/pallas_call | solution.py:227
  34.6 2.8 %product_coded.6.after = s16[3024,128]{1,0:T(8,128)(2,1)S(1)} custom-call(s32[2]{0:T(128)S(1)} %pad_add_fusion.others_1_.spot.place, bf16[672,2304]{1,0:T(8,128)(2,1)S(1)} %pack_left.2.left, bf16[16,2304,128]{2,1,0:T(8,128)(2,1)S(1)} %get-tuple-element.16.after.near, f32[672,256]{1,0:T(8,128)S(1)} %product_tails.2.tails.after, ...), custom_call_target="tpu_custom_call" | custom-call | flops 1000 | bytes 1000 | tf_op jit(solution)/shard_map/product_coded/pallas_call | solution.py:227
  37.4 2.6 %collective-permute-start.2 = (s16[3024,128]{1,0:T(8,128)(2,1)S(1)}, s16[3024,128]{1,0:T(8,128)(2,1)S(1)}, u32[]{:S(2)}, u32[]{:S(2)}) collective-permute-start(s16[3024,128]{1,0:T(8,128)(2,1)S(1)} %product_coded.6.after), channel_id=1, source_target_pairs={{0,12},{1,13},{2,14},{3,15},{4,0},{5,1},{6,2},{7,3},{8,4},{9,5},{1... | collective-permute-start | bytes 2322440 | tf_op jit(solution)/shard_map/ppermute | solution.py:294
  40.0 4.9 %pack_left.3.left = bf16[432,2304]{1,0:T(8,128)(2,1)S(1)} custom-call(bf16[16,16,128]{2,1,0:T(8,128)(2,1)S(1)} %broadcast_in_dim.21.others_0_.mask, bf16[8,138,16,138]{3,2,1,0:T(8,128)(2,1)} %bitcast.39, s16[3024,128]{1,0:T(8,128)(2,1)S(1)} %product_coded.6.after), custom_call_target="tpu_custom_call" | custom-call | flops 1000 | bytes 1000 | tf_op jit(solution)/shard_map/pack_left/pallas_call | solution.py:68
  46.1 2.1 %product_coded.11 = s16[1952,128]{1,0:T(8,128)(2,1)S(1)} custom-call(s32[2]{0:T(128)S(1)} %pad_add_fusion.others_1_.spot.place, bf16[432,2304]{1,0:T(8,128)(2,1)S(1)} %pack_left.3.left, bf16[16,2304,128]{2,1,0:T(8,128)(2,1)S(1)} %get-tuple-element.16.after.near, f32[432,256]{1,0:T(8,128)S(1)} %product_tails.3.tails.after, ...), custom_call_target="tpu_custom_call" | custom-call | flops 1000 | bytes 1000 | tf_op jit(solution)/shard_map/product_coded/pallas_call | solution.py:227
  48.2 4.0 %collective-permute-start.7 = (s16[1952,128]{1,0:T(8,128)(2,1)S(1)}, s16[1952,128]{1,0:T(8,128)(2,1)S(1)}, u32[]{:S(2)}, u32[]{:S(2)}) collective-permute-start(s16[1952,128]{1,0:T(8,128)(2,1)S(1)} %product_coded.11), channel_id=1, source_target_pairs={{0,2},{1,3},{2,0},{3,1},{4,6},{5,7},{6,4},{7,5},{8,10},{9,11},{10,... | collective-permute-start | bytes 1499144 | tf_op jit(solution)/shard_map/ppermute | solution.py:294
  57.4 2.5 %collective-permute-start.8 = (s16[1952,128]{1,0:T(8,128)(2,1)S(1)}, s16[1952,128]{1,0:T(8,128)(2,1)S(1)}, u32[]{:S(2)}, u32[]{:S(2)}) collective-permute-start(s16[1952,128]{1,0:T(8,128)(2,1)S(1)} %product_coded.7.after), channel_id=1, source_target_pairs={{0,3},{1,0},{2,1},{3,2},{4,7},{5,4},{6,5},{7,6},{8,11},{9,8},{10,9... | collective-permute-start | bytes 1499144 | tf_op jit(solution)/shard_map/ppermute | solution.py:294
  59.9 2.3 %product_own.2.after.own = f32[3024,128]{1,0:T(8,128)S(1)} custom-call(s32[2]{0:T(128)S(1)} %pad_add_fusion.others_1_.spot.place, bf16[672,2304]{1,0:T(8,128)(2,1)S(1)} %pack_left.2.left, bf16[16,2304,128]{2,1,0:T(8,128)(2,1)S(1)} %get-tuple-element.16.after.near, f32[672,256]{1,0:T(8,128)S(1)} %product_tails.2.tails.after, ...), custom_call_target="tpu_custom_call" | custom-call | flops 1000 | bytes 1000 | tf_op jit(solution)/shard_map/product_own/pallas_call | solution.py:227
  65.3 2.1 %merge.2 = (f32[768,128]{1,0:T(8,128)S(1)}, s16[768,128]{1,0:T(8,128)(2,1)S(1)}, s16[768,128]{1,0:T(8,128)(2,1)S(1)}, s16[768,128]{1,0:T(8,128)(2,1)S(1)}) custom-call(s32[2]{0:T(128)S(1)} %pad_add_fusion.others_1_.spot.place, f32[3024,128]{1,0:T(8,128)S(1)} %product_own.2.after.own, s16[3024,128]{1,0:T(8,128)(2,1)S(1)} %collective-permute-done.in1, ...), custom_call_target="tpu_custom_call" | custom-call | flops 1000 | bytes 1000 | tf_op jit(solution)/shard_map/merge/pallas_call | solution.py:277
  67.5 4.0 %collective-permute-start.3 = (s16[768,128]{1,0:T(8,128)(2,1)S(1)}, s16[768,128]{1,0:T(8,128)(2,1)S(1)}, u32[]{:S(2)}, u32[]{:S(2)}) collective-permute-start(s16[768,128]{1,0:T(8,128)(2,1)S(1)} %get-tuple-element.19), channel_id=1, source_target_pairs={{0,2},{1,3},{2,0},{3,1},{4,6},{5,7},{6,4},{7,5},{8,10},{9,11},{10,... | collective-permute-start | bytes 589832 | tf_op jit(solution)/shard_map/ppermute | solution.py:294
  72.4 2.2 %collective-permute-start.5 = (s16[768,128]{1,0:T(8,128)(2,1)S(1)}, s16[768,128]{1,0:T(8,128)(2,1)S(1)}, u32[]{:S(2)}, u32[]{:S(2)}) collective-permute-start(s16[768,128]{1,0:T(8,128)(2,1)S(1)} %get-tuple-element.21), channel_id=1, source_target_pairs={{0,3},{1,0},{2,1},{3,2},{4,7},{5,4},{6,5},{7,6},{8,11},{9,8},{10,9... | collective-permute-start | bytes 589832 | tf_op jit(solution)/shard_map/ppermute | solution.py:294
  77.7 2.9 %collective-permute-start.11 = (s16[496,128]{1,0:T(8,128)(2,1)S(1)}, s16[496,128]{1,0:T(8,128)(2,1)S(1)}, u32[]{:S(2)}, u32[]{:S(2)}) collective-permute-start(s16[496,128]{1,0:T(8,128)(2,1)S(1)} %get-tuple-element.26), channel_id=1, source_target_pairs={{0,12},{1,13},{2,14},{3,15},{4,0},{5,1},{6,2},{7,3},{8,4},{9,5},{1... | collective-permute-start | bytes 380936 | tf_op jit(solution)/shard_map/ppermute | solution.py:294
  82.7 10.2 %collocate.2 = (bf16[84,8,138]{2,1,0:T(8,128)(2,1)S(1)}, f32[16,8,1024]{2,1,0:T(8,128)S(1)}) custom-call(f32[8,128]{1,0:T(8,128)S(1)} %broadcast_in_dim.20.others_4_.keep, f32[8,128]{1,0:T(8,128)S(1)} %concatenate.6.others_3_.ids, f32[768,128]{1,0:T(8,128)S(1)} %get-tuple-element.18.after.own, s16[768,128]{1,0:T(8,128)(2,1)S(1)} %collective-permute-done.3.in1, ...), custom_call_target="tpu_custom_call" | custom-call | flops 1000 | bytes 1000 | tf_op jit(solution)/shard_map/collocate/pallas_call | solution.py:402
  92.9 8.3 %collocate.3 = (bf16[54,8,138]{2,1,0:T(8,128)(2,1)S(1)}, f32[16,8,1152]{2,1,0:T(8,128)}) custom-call(f32[8,128]{1,0:T(8,128)S(1)} %broadcast_in_dim.20.others_4_.keep, f32[8,128]{1,0:T(8,128)S(1)} %concatenate.6.others_3_.ids, f32[496,128]{1,0:T(8,128)S(1)} %get-tuple-element.22.after.own, s16[496,128]{1,0:T(8,128)(2,1)S(1)} %collective-permute-done.9.in1, ...), custom_call_target="tpu_custom_call" | custom-call | flops 1000 | bytes 1000 | tf_op jit(solution)/shard_map/collocate/pallas_call | solution.py:402
  101.3 6.7 %all-to-all-start = ((f32[16,8,1152]{2,1,0:T(8,128)}), f32[16,8,1152]{2,1,0:T(8,128)S(1)}, u32[]{:S(2)}, u32[]{:S(2)}) async-start(f32[16,8,1152]{2,1,0:T(8,128)} %get-tuple-element.29), calls=%async_computation | async-start | bytes 1179648 | tf_op jit(solution)/shard_map/all_to_all | solution.py:520
  108.0 10.6 %all-to-all-done.points = f32[16,8,1152]{2,1,0:T(8,128)S(1)} async-done(((f32[16,8,1152]{2,1,0:T(8,128)}), f32[16,8,1152]{2,1,0:T(8,128)S(1)}, u32[]{:S(2)}, u32[]{:S(2)}) %all-to-all-start) | async-done | bytes 589856 | tf_op jit(solution)/shard_map/all_to_all | solution.py:520
  122.5 2.7 %collective-permute-start.14 = (f32[16,1024]{1,0:T(8,128)S(1)}, f32[16,1024]{1,0:T(8,128)S(1)}, u32[]{:S(2)}, u32[]{:S(2)}) collective-permute-start(f32[16,1024]{1,0:T(8,128)S(1)} %get-tuple-element.31), channel_id=1, source_target_pairs={{0,64},{16,80},{32,96},{48,112},{64,0},{80,16},{96,32},{112,48},{1... | collective-permute-start | bytes 196616 | tf_op jit(solution)/shard_map/ppermute | solution.py:498
  126.7 2.1 %collective-permute-done.14.in2 = f32[16,1024]{1,0:T(8,128)S(1)} collective-permute-done((f32[16,1024]{1,0:T(8,128)S(1)}, f32[16,1024]{1,0:T(8,128)S(1)}, u32[]{:S(2)}, u32[]{:S(2)}) %collective-permute-start.14) | collective-permute-done | bytes 65568 | tf_op jit(solution)/shard_map/ppermute | solution.py:498
  131.5 3.5 %all-to-all-start.1 = ((f32[16,8,128]{2,1,0:T(8,128)}), f32[16,8,128]{2,1,0:T(8,128)S(1)}, u32[]{:S(2)}, u32[]{:S(2)}) async-start(f32[16,8,128]{2,1,0:T(8,128)} %filter_rows.1), calls=%async_computation.1 | async-start | bytes 131072 | tf_op jit(solution)/shard_map/all_to_all | solution.py:523
  135.9 6.7 %all-to-all-done.1 = f32[16,8,128]{2,1,0:T(8,128)S(1)} async-done(((f32[16,8,128]{2,1,0:T(8,128)}), f32[16,8,128]{2,1,0:T(8,128)S(1)}, u32[]{:S(2)}, u32[]{:S(2)}) %all-to-all-start.1) | async-done | bytes 65568 | tf_op jit(solution)/shard_map/all_to_all | solution.py:523
  (63 shorter events, 30.5 us)
Async XLA Ops:
  27.7 29.7 %collective-permute-start.1 = (s16[3024,128]{1,0:T(8,128)(2,1)S(1)}, s16[3024,128]{1,0:T(8,128)(2,1)S(1)}, u32[]{:S(2)}, u32[]{:S(2)}) collective-permute-start(s16[3024,128]{1,0:T(8,128)(2,1)S(1)} %product_coded.9), channel_id=1, source_target_pairs={{0,8},{1,9},{2,10},{3,11},{4,12},{5,13},{6,14},{7,15},{8,0},{9,1},... | collective-permute-start | bytes 2322440 | tf_op jit(solution)/shard_map/ppermute | solution.py:294
  33.8 31.1 %collective-permute-start = (s16[3024,128]{1,0:T(8,128)(2,1)S(1)}, s16[3024,128]{1,0:T(8,128)(2,1)S(1)}, u32[]{:S(2)}, u32[]{:S(2)}) collective-permute-start(s16[3024,128]{1,0:T(8,128)(2,1)S(1)} %product_coded.8), channel_id=1, source_target_pairs={{0,4},{1,5},{2,6},{3,7},{4,8},{5,9},{6,10},{7,11},{8,12},{9,13},{1... | collective-permute-start | bytes 2322440 | tf_op jit(solution)/shard_map/ppermute | solution.py:294
  37.4 28.0 %collective-permute-start.2 = (s16[3024,128]{1,0:T(8,128)(2,1)S(1)}, s16[3024,128]{1,0:T(8,128)(2,1)S(1)}, u32[]{:S(2)}, u32[]{:S(2)}) collective-permute-start(s16[3024,128]{1,0:T(8,128)(2,1)S(1)} %product_coded.6.after), channel_id=1, source_target_pairs={{0,12},{1,13},{2,14},{3,15},{4,0},{5,1},{6,2},{7,3},{8,4},{9,5},{1... | collective-permute-start | bytes 2322440 | tf_op jit(solution)/shard_map/ppermute | solution.py:294
  48.2 24.2 %collective-permute-start.7 = (s16[1952,128]{1,0:T(8,128)(2,1)S(1)}, s16[1952,128]{1,0:T(8,128)(2,1)S(1)}, u32[]{:S(2)}, u32[]{:S(2)}) collective-permute-start(s16[1952,128]{1,0:T(8,128)(2,1)S(1)} %product_coded.11), channel_id=1, source_target_pairs={{0,2},{1,3},{2,0},{3,1},{4,6},{5,7},{6,4},{7,5},{8,10},{9,11},{10,... | collective-permute-start | bytes 1499144 | tf_op jit(solution)/shard_map/ppermute | solution.py:294
  54.2 20.8 %collective-permute-start.6 = (s16[1952,128]{1,0:T(8,128)(2,1)S(1)}, s16[1952,128]{1,0:T(8,128)(2,1)S(1)}, u32[]{:S(2)}, u32[]{:S(2)}) collective-permute-start(s16[1952,128]{1,0:T(8,128)(2,1)S(1)} %product_coded.10), channel_id=1, source_target_pairs={{0,1},{1,2},{2,3},{3,0},{4,5},{5,6},{6,7},{7,4},{8,9},{9,10},{10,1... | collective-permute-start | bytes 1499144 | tf_op jit(solution)/shard_map/ppermute | solution.py:294
  57.4 18.3 %collective-permute-start.8 = (s16[1952,128]{1,0:T(8,128)(2,1)S(1)}, s16[1952,128]{1,0:T(8,128)(2,1)S(1)}, u32[]{:S(2)}, u32[]{:S(2)}) collective-permute-start(s16[1952,128]{1,0:T(8,128)(2,1)S(1)} %product_coded.7.after), channel_id=1, source_target_pairs={{0,3},{1,0},{2,1},{3,2},{4,7},{5,4},{6,5},{7,6},{8,11},{9,8},{10,9... | collective-permute-start | bytes 1499144 | tf_op jit(solution)/shard_map/ppermute | solution.py:294
  67.5 13.1 %collective-permute-start.3 = (s16[768,128]{1,0:T(8,128)(2,1)S(1)}, s16[768,128]{1,0:T(8,128)(2,1)S(1)}, u32[]{:S(2)}, u32[]{:S(2)}) collective-permute-start(s16[768,128]{1,0:T(8,128)(2,1)S(1)} %get-tuple-element.19), channel_id=1, source_target_pairs={{0,2},{1,3},{2,0},{3,1},{4,6},{5,7},{6,4},{7,5},{8,10},{9,11},{10,... | collective-permute-start | bytes 589832 | tf_op jit(solution)/shard_map/ppermute | solution.py:294
  71.4 10.4 %collective-permute-start.4 = (s16[768,128]{1,0:T(8,128)(2,1)S(1)}, s16[768,128]{1,0:T(8,128)(2,1)S(1)}, u32[]{:S(2)}, u32[]{:S(2)}) collective-permute-start(s16[768,128]{1,0:T(8,128)(2,1)S(1)} %get-tuple-element.20), channel_id=1, source_target_pairs={{0,1},{1,2},{2,3},{3,0},{4,5},{5,6},{6,7},{7,4},{8,9},{9,10},{10,1... | collective-permute-start | bytes 589832 | tf_op jit(solution)/shard_map/ppermute | solution.py:294
  72.4 10.2 %collective-permute-start.5 = (s16[768,128]{1,0:T(8,128)(2,1)S(1)}, s16[768,128]{1,0:T(8,128)(2,1)S(1)}, u32[]{:S(2)}, u32[]{:S(2)}) collective-permute-start(s16[768,128]{1,0:T(8,128)(2,1)S(1)} %get-tuple-element.21), channel_id=1, source_target_pairs={{0,3},{1,0},{2,1},{3,2},{4,7},{5,4},{6,5},{7,6},{8,11},{9,8},{10,9... | collective-permute-start | bytes 589832 | tf_op jit(solution)/shard_map/ppermute | solution.py:294
  77.3 15.6 %collective-permute-start.10 = (s16[496,128]{1,0:T(8,128)(2,1)S(1)}, s16[496,128]{1,0:T(8,128)(2,1)S(1)}, u32[]{:S(2)}, u32[]{:S(2)}) collective-permute-start(s16[496,128]{1,0:T(8,128)(2,1)S(1)} %get-tuple-element.25), channel_id=1, source_target_pairs={{0,4},{1,5},{2,6},{3,7},{4,8},{5,9},{6,10},{7,11},{8,12},{9,13},{1... | collective-permute-start | bytes 380936 | tf_op jit(solution)/shard_map/ppermute | solution.py:294
  77.7 15.2 %collective-permute-start.11 = (s16[496,128]{1,0:T(8,128)(2,1)S(1)}, s16[496,128]{1,0:T(8,128)(2,1)S(1)}, u32[]{:S(2)}, u32[]{:S(2)}) collective-permute-start(s16[496,128]{1,0:T(8,128)(2,1)S(1)} %get-tuple-element.26), channel_id=1, source_target_pairs={{0,12},{1,13},{2,14},{3,15},{4,0},{5,1},{6,2},{7,3},{8,4},{9,5},{1... | collective-permute-start | bytes 380936 | tf_op jit(solution)/shard_map/ppermute | solution.py:294
  80.6 12.3 %collective-permute-start.9 = (s16[496,128]{1,0:T(8,128)(2,1)S(1)}, s16[496,128]{1,0:T(8,128)(2,1)S(1)}, u32[]{:S(2)}, u32[]{:S(2)}) collective-permute-start(s16[496,128]{1,0:T(8,128)(2,1)S(1)} %get-tuple-element.24), channel_id=1, source_target_pairs={{0,8},{1,9},{2,10},{3,11},{4,12},{5,13},{6,14},{7,15},{8,0},{9,1},... | collective-permute-start | bytes 380936 | tf_op jit(solution)/shard_map/ppermute | solution.py:294
  92.9 36.6 %copy-start.1 = (f32[256,256]{1,0:T(8,128)S(1)}, f32[256,256]{1,0:T(8,128)}, u32[]{:S(2)}) copy-start(f32[256,256]{1,0:T(8,128)} %constant.115.clone.second) | copy-start | bytes 786436
  92.9 36.6 %copy-start.2 = (f32[256,256]{1,0:T(8,128)S(1)}, f32[256,256]{1,0:T(8,128)}, u32[]{:S(2)}) copy-start(f32[256,256]{1,0:T(8,128)} %constant.116.clone.third) | copy-start | bytes 786436
  92.9 36.6 %copy-start.3 = (f32[256,128]{1,0:T(8,128)S(1)}, f32[256,128]{1,0:T(8,128)}, u32[]{:S(2)}) copy-start(f32[256,128]{1,0:T(8,128)} %constant.114.clone.first) | copy-start | bytes 393220
  92.9 36.6 %copy-start.4 = (f32[128,256]{1,0:T(8,128)S(1)}, f32[128,256]{1,0:T(8,128)}, u32[]{:S(2)}) copy-start(f32[128,256]{1,0:T(8,128)} %constant.117.clone.last) | copy-start | bytes 393220
  92.9 36.6 %copy-start.5 = (f32[128,128]{1,0:T(8,128)S(1)}, f32[128,128]{1,0:T(8,128)}, u32[]{:S(2)}) copy-start(f32[128,128]{1,0:T(8,128)} %constant.118.clone.tc) | copy-start | bytes 196612
  92.9 36.6 %copy-start.6 = (f32[128,128]{1,0:T(8,128)S(1)}, f32[128,128]{1,0:T(8,128)}, u32[]{:S(2)}) copy-start(f32[128,128]{1,0:T(8,128)} %constant.119.clone.ts) | copy-start | bytes 196612
  101.3 17.3 %all-to-all-start = ((f32[16,8,1152]{2,1,0:T(8,128)}), f32[16,8,1152]{2,1,0:T(8,128)S(1)}, u32[]{:S(2)}, u32[]{:S(2)}) async-start(f32[16,8,1152]{2,1,0:T(8,128)} %get-tuple-element.29), calls=%async_computation | async-start | bytes 1179648 | tf_op jit(solution)/shard_map/all_to_all | solution.py:520
  119.3 1.6 %collective-permute-start.12 = (f32[4,16,1024]{2,1,0:T(8,128)S(1)}, f32[4,16,1024]{2,1,0:T(8,128)S(1)}, u32[]{:S(2)}, u32[]{:S(2)}) collective-permute-start(f32[4,16,1024]{2,1,0:T(8,128)S(1)} %dynamic-slice_bitcast_fusion), channel_id=1, source_target_pairs={{0,16},{16,0},{32,48},{48,32},{64,80},{80,64},{96,112},{112,96},{1... | collective-permute-start | bytes 786440 | tf_op jit(solution)/shard_map/ppermute | solution.py:494
  120.9 5.7 %collective-permute-start.13 = (f32[16,1024]{1,0:T(8,128)S(1)}, f32[16,1024]{1,0:T(8,128)S(1)}, u32[]{:S(2)}, u32[]{:S(2)}) collective-permute-start(f32[16,1024]{1,0:T(8,128)S(1)} %get-tuple-element.32), channel_id=1, source_target_pairs={{0,32},{16,48},{32,64},{48,80},{64,96},{80,112},{96,0},{112,16},{1... | collective-permute-start | bytes 196616 | tf_op jit(solution)/shard_map/ppermute | solution.py:498
  122.5 6.2 %collective-permute-start.14 = (f32[16,1024]{1,0:T(8,128)S(1)}, f32[16,1024]{1,0:T(8,128)S(1)}, u32[]{:S(2)}, u32[]{:S(2)}) collective-permute-start(f32[16,1024]{1,0:T(8,128)S(1)} %get-tuple-element.31), channel_id=1, source_target_pairs={{0,64},{16,80},{32,96},{48,112},{64,0},{80,16},{96,32},{112,48},{1... | collective-permute-start | bytes 196616 | tf_op jit(solution)/shard_map/ppermute | solution.py:498
  125.2 4.3 %collective-permute-start.15 = (f32[16,1024]{1,0:T(8,128)S(1)}, f32[16,1024]{1,0:T(8,128)S(1)}, u32[]{:S(2)}, u32[]{:S(2)}) collective-permute-start(f32[16,1024]{1,0:T(8,128)S(1)} %get-tuple-element.30), channel_id=1, source_target_pairs={{0,96},{16,112},{32,0},{48,16},{64,32},{80,48},{96,64},{112,80},{1... | collective-permute-start | bytes 196616 | tf_op jit(solution)/shard_map/ppermute | solution.py:498
  131.5 11.1 %all-to-all-start.1 = ((f32[16,8,128]{2,1,0:T(8,128)}), f32[16,8,128]{2,1,0:T(8,128)S(1)}, u32[]{:S(2)}, u32[]{:S(2)}) async-start(f32[16,8,128]{2,1,0:T(8,128)} %filter_rows.1), calls=%async_computation.1 | async-start | bytes 131072 | tf_op jit(solution)/shard_map/all_to_all | solution.py:523
  (1 other events, 7.0 us)
where the time goes:
time: 144 us; the launch traced here: 143 us
  Pallas kernels  70 us (49%)
  starting transfers between devices  41.3 us (29%)
  waiting for transfers between devices  25.5 us (18%)
  local copies, waits for them, and re-layouts  2.95 us (2%)
  other arithmetic  2.37 us (2%)
    ppermute x12, starting transfers between devices, send(): return lax.ppermute(array, 'col', turn(d, 0) if axis == 0 else turn(0, d))  25.4 us
    pallas_call x8, Pallas kernels, product_group(): pl.pallas_call(functools.partial(product_kernel, half, d), in_specs=[pl.B...  18.6 us
    pallas_call x2, Pallas kernels, collocate(): pl.pallas_call(functools.partial(collocate_kernel, half), in_specs=[vmem]...  18.5 us
    pallas_call x1, Pallas kernels, pack_right(): pl.pallas_call(pack_right_kernel, grid=(8,), in_specs=[pl.BlockSpec((2, B...  12.5 us
    pallas_call x2, Pallas kernels, pack_left(): pl.pallas_call(functools.partial(pack_left_kernel, count // 2), grid=(ROW...  11.9 us
    all_to_all x1, waiting for transfers between devices, shards(): lax.all_to_all(points, 'col', split_axis=0, concat_axis=0, tiled=True)  10.6 us
    all_to_all x1, waiting for transfers between devices, shards(): lax.all_to_all(filtered, 'col', split_axis=0, concat_axis=0, tiled=True)  6.71 us
    all_to_all x1, starting transfers between devices, shards(): lax.all_to_all(points, 'col', split_axis=0, concat_axis=0, tiled=True)  6.68 us
  transfers between devices with their start and end apart: 18, of which 11 were waited for; matrix products, arithmetic and copies ran while one was open for 1% of the time, Pallas kernels for 25%

commit v1 on v0

--- a/solution.py
+++ b/solution.py
@@ -23,6 +23,7 @@
 FOLD = (96, 64)
 STEP = (28, 18)
 POINTS = 2048
+EARLY = 56
 
 
 def in_hbm(array):
@@ -43,7 +44,14 @@
         out(half, rest.astype(BF16))
 
 
-def pack_left_kernel(pairs, mask, blocks, after, out):
+def pack_left_kernel(pairs, pattern, blocks, after, out, mask):
+    @pl.when(pl.program_id(0) == 0)
+    def _():
+        kept = pattern[...].astype(F32)
+        for k in range(16):
+            column = jnp.broadcast_to(kept[:, k : k + 1], (8, 128))
+            mask[k] = jnp.concatenate([column, column], axis=0).astype(BF16)
+
     def step(p, carry):
         pair = jnp.transpose(blocks[:, pl.ds(2 * p, 2)], (1, 0, 2, 3)).reshape(16, 16, BS)
         wide = jnp.swapaxes(pair, 0, 1)
@@ -63,13 +71,13 @@
     lax.fori_loop(0, pairs, step, 0)
 
 
-def pack_left(half, mask, blocks, after):
+def pack_left(half, pattern, blocks, after):
     count = STEP[half]
     return pl.pallas_call(
         functools.partial(pack_left_kernel, count // 2),
         grid=(ROWS[half] // 8 // count,),
         in_specs=[
-            pl.BlockSpec((16, 16, 128), lambda g: (0, 0, 0)),
+            pl.BlockSpec((8, 16), lambda g: (0, 0)),
             pl.BlockSpec(
                 (pl.Element(8), pl.Element(count), pl.Element(16), pl.Element(BS)),
                 lambda g: (0, CUT[half] // 8 + count * g, 0, 0),
@@ -78,10 +86,11 @@
         ],
         out_specs=pl.BlockSpec((count * 8, WIDE), lambda g: (g, 0)),
         out_shape=pltpu.VMEM((ROWS[half], WIDE), BF16),
+        scratch_shapes=[pltpu.VMEM((16, 16, 128), BF16)],
         compiler_params=pltpu.CompilerParams(vmem_limit_bytes=32 * MIB),
         cost_estimate=pl.CostEstimate(flops=1000, bytes_accessed=1000, transcendentals=0),
         name="pack_left",
-    )(mask, in_hbm(blocks), after)
+    )(pattern, in_hbm(blocks), after)
 
 
 def pack_right_kernel(blocks, *others):
@@ -294,17 +303,14 @@
     return lax.ppermute(array, "col", turn(d, 0) if axis == 0 else turn(0, d))
 
 
-def exchange_products(blocks_a, pattern, blocks_b, before):
-    place = lax.axis_index("col").astype(jnp.int32)
-    spot = jnp.stack([place // 4, place % 4])
-    mask = jnp.broadcast_to(jnp.tile(pattern.T, (1, 2))[:, :, None], (16, 16, 128)).astype(BF16)
+def exchange_products(spot, blocks_a, pattern, blocks_b, by_point, before):
     blocks_a = jnp.transpose(blocks_a, (0, 2, 1, 3))
-    near, rest = pack_right(jnp.transpose(blocks_b, (0, 2, 1, 3)), [mask, spot] + before)
+    near, rest = pack_right(jnp.transpose(blocks_b, (0, 2, 1, 3)), [spot] + before)
     after = near
     parts, owns = ([], []), []
     lefts = []
     for half in range(2):
-        left = pack_left(half, mask, blocks_a, after)
+        left = pack_left(half, pattern, blocks_a, after)
         tails = product_tails(half, left, rest, after)
         lefts.append((left, near, tails))
         after = tails
@@ -316,29 +322,49 @@
         after = product_group(half, 0, spot, *lefts[half], after)
         owns.append(after)
 
+    early, after = fetch(by_point, after)
+
     def finish(half, after):
         mine, *outs = merge(half, spot, owns[half], parts[half], after)
         return mine, [send(outs[d - 1], 1 - half, d) for d in (2, 1, 3)]
 
-    return finish, after
-
-
-def collocate_kernel(half, keep, ids, own, in1, in2, in3, cols, rows, after, *rest):
+    return finish, early, after
+
+
+def fetch_kernel(rows, after, out, done, sem):
+    copy = pltpu.make_async_copy(rows.at[pl.ds(0, EARLY)], out, sem)
+    copy.start()
+    done[...] = jnp.zeros((8, 128), F32)
+    copy.wait()
+
+
+def fetch(rows, after):
+    vmem = pl.BlockSpec(memory_space=pltpu.VMEM)
+    return pl.pallas_call(
+        fetch_kernel,
+        in_specs=[pl.BlockSpec(memory_space=pltpu.HBM), pl.BlockSpec(memory_space=pl.ANY)],
+        out_specs=[vmem, vmem],
+        out_shape=[pltpu.VMEM((EARLY, 8, 16384), BF16), jax.ShapeDtypeStruct((8, 128), F32)],
+        scratch_shapes=[pltpu.SemaphoreType.DMA],
+        compiler_params=pltpu.CompilerParams(vmem_limit_bytes=20 * MIB),
+        cost_estimate=pl.CostEstimate(flops=1000, bytes_accessed=1000, transcendentals=0),
+        name="fetch",
+    )(in_hbm(rows), after)
+
+
+def collocate_kernel(half, spot, keep, ids, own, in1, in2, in3, cols, rows, after, *rest):
     size = FOLD[half]
-    if half == 0:
-        density, out, stacked, right, held, held_cols, sems = rest
-        before = None
-    else:
-        before, density, out, stacked, right, held, held_cols, sems = rest
+    before, density, out, stacked, right, held, held_cols, sems = rest
     count = ROWS[half]
+    first = EARLY if half == 0 else 0
     tiles = 16384 // POINTS
 
     def copies(g):
-        spot = pl.ds(pl.multiple_of(g * POINTS, POINTS), POINTS)
+        span = pl.ds(pl.multiple_of(g * POINTS, POINTS), POINTS)
         return (
-            pltpu.make_async_copy(cols.at[0, :, spot], held_cols.at[g], sems.at[0, g]),
+            pltpu.make_async_copy(cols.at[0, :, span], held_cols.at[g], sems.at[0, g]),
             pltpu.make_async_copy(
-                rows.at[pl.ds(CUT[half] // 8, count // 8), :, spot], held.at[g], sems.at[1, g]
+                rows.at[pl.ds(CUT[half] // 8 + first, count // 8 - first), :, span], held.at[g], sems.at[1, g]
             ),
         )
 
@@ -359,7 +385,11 @@
                 shift = (128 - 16 * (q + base)) % 128
                 tails.append(pltpu.roll(piece, shift, 1) if shift else piece)
         tail = jnp.where(lanes(count) < BS - 128, jnp.concatenate(tails, axis=0), 0.0)
-        kept = keep[...][None]
+        row = lax.broadcasted_iota(jnp.int32, (8, 128), 0)
+        kept = jnp.zeros((8, 128), F32)
+        for i in range(8):
+            kept = jnp.where(row == i, keep[i].astype(F32), kept)
+        kept = kept[None]
         main = (main.reshape(count // 8, 8, 128) * kept).reshape(count, 128).astype(BF16)
         tail = (tail.reshape(count // 8, 8, 128) * kept).reshape(count, 128).astype(BF16)
         stacked[:, 0:128] = main
@@ -382,34 +412,44 @@
         for t in range(POINTS // 256):
             here = slice(t * 256, (t + 1) * 256)
             inner = jnp.dot(stacked[...], right[:, here], preferred_element_type=F32).reshape(count // 8, 8, 256)
-            total = jnp.sum(inner * held[g, :, :, here].astype(F32), axis=0)
+            total = jnp.sum(inner[first:] * held[g, :, :, here].astype(F32), axis=0)
+            if half == 0:
+                at = pl.ds(pl.multiple_of(g * POINTS + t * 256, 256), 256)
+                total = total + jnp.sum(inner[:first] * before[:, :, at].astype(F32), axis=0)
             within = slice(t % 4 * 256, t % 4 * 256 + 256)
             if half == 1:
                 total = total + before[per * g + t // 4, :, within]
             out[per * g + t // 4, :, within] = total
         if half == 1:
+            row = lax.broadcasted_iota(jnp.int32, (8, 128), 0)
+            label = jnp.zeros((8, 128), F32)
+            for i in range(8):
+                here = (row == 0) & (lanes(8) == 32 * spot[0] + 8 * spot[1] + i)
+                label = jnp.where(here, ids[i].astype(F32), label)
             for n in range(POINTS // 1024):
-                out[per * g + n, :, 1024:1152] = ids[...]
+                out[per * g + n, :, 1024:1152] = label
 
     lax.fori_loop(0, tiles, step, 0)
 
 
-def collocate(half, keep, ids, own, parts, basis_cols, basis_rows, before, after):
+def collocate(half, spot, keep, ids, own, parts, basis_cols, basis_rows, before, after):
     count = ROWS[half]
     wide = 1152 if half else 1024
     vmem = pl.BlockSpec(memory_space=pltpu.VMEM)
+    first = EARLY if half == 0 else 0
     tiles = 16384 // POINTS
     return pl.pallas_call(
         functools.partial(collocate_kernel, half),
-        in_specs=[vmem] * 6
+        in_specs=[pl.BlockSpec(memory_space=pltpu.SMEM)] * 3
+        + [vmem] * 4
         + [pl.BlockSpec(memory_space=pltpu.HBM)] * 2
         + [pl.BlockSpec(memory_space=pl.ANY)]
-        + [vmem] * half,
+        + [vmem],
         out_specs=[vmem] * 2,
         scratch_shapes=[
             pltpu.VMEM((count, 256), BF16),
             pltpu.VMEM((256, POINTS), BF16),
-            pltpu.VMEM((tiles, count // 8, 8, POINTS), BF16),
+            pltpu.VMEM((tiles, count // 8 - first, 8, POINTS), BF16),
             pltpu.VMEM((tiles, BS, POINTS), BF16),
             pltpu.SemaphoreType.DMA((2, tiles)),
         ],
@@ -417,10 +457,10 @@
             jax.ShapeDtypeStruct((count // 8, 8, BS), BF16),
             jax.ShapeDtypeStruct((16, 8, wide), F32),
         ],
-        compiler_params=pltpu.CompilerParams(vmem_limit_bytes=(38, 28)[half] * MIB),
+        compiler_params=pltpu.CompilerParams(vmem_limit_bytes=(24, 28)[half] * MIB),
         cost_estimate=pl.CostEstimate(flops=1000, bytes_accessed=1000, transcendentals=0),
         name="collocate",
-    )(keep, ids, own, *parts, in_hbm(basis_cols), in_hbm(basis_rows), after, *before)
+    )(spot, keep, ids, own, *parts, in_hbm(basis_cols), in_hbm(basis_rows), after, *before)
 
 
 def bricks_kernel(points, out):
@@ -501,19 +541,20 @@
 
 def shards(blocks_a, pattern_a, blocks_b, filter_mask, task_brick, basis_rows, basis_cols, kernel):
     kern = jnp.transpose(kernel.reshape(8, 128, 16), (0, 2, 1)).reshape(128, 128)
-    lane = jnp.arange(128, dtype=jnp.int32)
-    owners = jnp.where(lane // 8 == lax.axis_index("col"), jnp.tile(task_brick.reshape(8), 16), 0)
-    ids = jnp.concatenate([owners.astype(F32)[None], jnp.zeros((7, 128), F32)], axis=0)
-    keep = jnp.broadcast_to(filter_mask.reshape(8, 1).astype(F32), (8, 128))
+    place = lax.axis_index("col").astype(jnp.int32)
+    spot = jnp.stack([place // 4, place % 4])
+    keep, ids = filter_mask.reshape(8), task_brick.reshape(8)
     by_point = jnp.transpose(basis_rows, (1, 0, 2))
-    finish, after = exchange_products(blocks_a, pattern_a, blocks_b, [kern, ids, keep])
+    finish, early, after = exchange_products(spot, blocks_a, pattern_a, blocks_b, by_point, [kern])
     densities, before, sums = [], [], []
     for half in range(2):
         sums.append(finish(half, after))
         after = sums[half][0]
     for half in range(2):
         own, parts = sums[half]
-        density, after = collocate(half, keep, ids, own, parts, basis_cols, by_point, before, after)
+        density, after = collocate(
+            half, spot, keep, ids, own, parts, basis_cols, by_point, [early] if half == 0 else before, after
+        )
         densities.append(density)
         before = [after]
     points = after

time: 144 us -> 146 us (1.014)
  Pallas kernels: 70 us -> 75.2 us
  waiting for transfers between devices: 25.5 us -> 21.6 us
  starting transfers between devices: 41.3 us -> 44.5 us
    ppermute x12, starting transfers between devices: 25.4 us -> 31.5 us  [send(): return lax.ppermute(array, 'col', turn(d, 0) if axis == 0 else turn(0, d))]
    pallas_call x2 -> x3, Pallas kernels: 18.5 us -> 23.6 us  [the longest x2 18.4 us: collocate(): pl.pallas_call(functools.partial(collocate_kernel, half), in_specs=[pl.Bl...]
    ppermute x12, waiting for transfers between devices: 3.88 us -> 0.21 us  [send(): return lax.ppermute(array, 'col', turn(d, 0) if axis == 0 else turn(0, d))]
    all_to_all x1, starting transfers between devices: 6.68 us -> 3.63 us  [shards(): lax.all_to_all(points, 'col', split_axis=0, concat_axis=0, tiled=True)]
  transfers between devices with their start and end apart: 18 -> 18, of which waited for: 11 -> 6; matrix products, arithmetic and copies ran while one was open for 1% -> 1% of each run, Pallas kernels for 25% -> 28%
where the time goes in v1:
time: 146 us; the launch traced here: 145 us
  Pallas kernels  75.2 us (52%)
  starting transfers between devices  44.5 us (30%)
  waiting for transfers between devices  21.6 us (15%)
  local copies, waits for them, and re-layouts  1.95 us (1%)
    ppermute x12, starting transfers between devices, send(): return lax.ppermute(array, 'col', turn(d, 0) if axis == 0 else turn(0, d))  31.5 us
    pallas_call x8, Pallas kernels, product_group(): pl.pallas_call(functools.partial(product_kernel, half, d), in_specs=[pl.B...  18.6 us
    pallas_call x2, Pallas kernels, collocate(): pl.pallas_call(functools.partial(collocate_kernel, half), in_specs=[pl.Bl...  18.4 us
    pallas_call x1, Pallas kernels, pack_right(): pl.pallas_call(pack_right_kernel, grid=(8,), in_specs=[pl.BlockSpec((2, B...  12.5 us
    pallas_call x2, Pallas kernels, pack_left(): pl.pallas_call(functools.partial(pack_left_kernel, count // 2), grid=(ROW...  12 us
    all_to_all x1, waiting for transfers between devices, shards(): lax.all_to_all(points, 'col', split_axis=0, concat_axis=0, tiled=True)  10.4 us
    all_to_all x1, waiting for transfers between devices, shards(): lax.all_to_all(filtered, 'col', split_axis=0, concat_axis=0, tiled=True)  6.71 us
    ppermute x3, starting transfers between devices, scatter_rows(): lax.ppermute(part, 'row', [(r, (r + 2 * d) % 8) for r in range(8)])  5.72 us
  transfers between devices with their start and end apart: 18, of which 6 were waited for; matrix products, arithmetic and copies ran while one was open for 1% of the time, Pallas kernels for 28%

profile of v1, /device:TPU:0, one launch (start us, length us, event | category | flops | bytes accessed | tf_op | source)
XLA Modules:
  0.0 145.3 jit_solution(18025637937709132195)
XLA Ops:
  1.9 12.5 %pack_right.1 = (bf16[16,2304,128]{2,1,0:T(8,128)(2,1)S(1)}, bf16[2304,256]{1,0:T(8,128)(2,1)S(1)}) custom-call(bf16[16,138,16,138]{3,2,1,0:T(8,128)(2,1)} %bitcast.40, s32[2]{0:T(128)S(1)} %pad_add_fusion.others_0_.spot.place, f32[128,128]{1,0:T(8,128)S(1)} %bitcast.29), custom_call_target="tpu_custom_call" | custom-call | flops 1000 | bytes 1000 | tf_op jit(solution)/shard_map/pack_right/pallas_call | solution.py:122
  14.5 7.0 %pack_left.2.left = bf16[672,2304]{1,0:T(8,128)(2,1)S(1)} custom-call(s32[8,16]{1,0:T(8,128)S(1)} %copy-done.7, bf16[8,138,16,138]{3,2,1,0:T(8,128)(2,1)} %bitcast.38, bf16[16,2304,128]{2,1,0:T(8,128)(2,1)S(1)} %get-tuple-element.18.after.near), custom_call_target="tpu_custom_call" | custom-call | flops 1000 | bytes 1000 | tf_op jit(solution)/shard_map/pack_left/pallas_call | solution.py:76
  22.5 2.8 %product_coded.8 = s16[3024,128]{1,0:T(8,128)(2,1)S(1)} custom-call(s32[2]{0:T(128)S(1)} %pad_add_fusion.others_0_.spot.place, bf16[672,2304]{1,0:T(8,128)(2,1)S(1)} %pack_left.2.left, bf16[16,2304,128]{2,1,0:T(8,128)(2,1)S(1)} %get-tuple-element.18.after.near, f32[672,256]{1,0:T(8,128)S(1)} %product_tails.2.tails.after, f32[672,256]{1,0:T(8,128)S(1)} %product_tails.2.tails.after), custom_call_target="tpu_custom_call" | custom-call | flops 1000 | bytes 1000 | tf_op jit(solution)/shard_map/product_coded/pallas_call | solution.py:236
  27.1 2.8 %product_coded.9 = s16[3024,128]{1,0:T(8,128)(2,1)S(1)} custom-call(s32[2]{0:T(128)S(1)} %pad_add_fusion.others_0_.spot.place, bf16[672,2304]{1,0:T(8,128)(2,1)S(1)} %pack_left.2.left, bf16[16,2304,128]{2,1,0:T(8,128)(2,1)S(1)} %get-tuple-element.18.after.near, f32[672,256]{1,0:T(8,128)S(1)} %product_tails.2.tails.after, f32[672,256]{1,0:T(8,128)S(1)} %product_tails.2.tails.after), custom_call_target="tpu_custom_call" | custom-call | flops 1000 | bytes 1000 | tf_op jit(solution)/shard_map/product_coded/pallas_call | solution.py:236
  29.8 3.0 %collective-permute-start.1 = (s16[3024,128]{1,0:T(8,128)(2,1)S(1)}, s16[3024,128]{1,0:T(8,128)(2,1)S(1)}, u32[]{:S(2)}, u32[]{:S(2)}) collective-permute-start(s16[3024,128]{1,0:T(8,128)(2,1)S(1)} %product_coded.9), channel_id=1, source_target_pairs={{0,8},{1,9},{2,10},{3,11},{4,12},{5,13},{6,14},{7,15},{8,0},{9,1},... | collective-permute-start | bytes 2322440 | tf_op jit(solution)/shard_map/ppermute | solution.py:303
  32.8 2.8 %product_coded.6.after = s16[3024,128]{1,0:T(8,128)(2,1)S(1)} custom-call(s32[2]{0:T(128)S(1)} %pad_add_fusion.others_0_.spot.place, bf16[672,2304]{1,0:T(8,128)(2,1)S(1)} %pack_left.2.left, bf16[16,2304,128]{2,1,0:T(8,128)(2,1)S(1)} %get-tuple-element.18.after.near, f32[672,256]{1,0:T(8,128)S(1)} %product_tails.2.tails.after, ...), custom_call_target="tpu_custom_call" | custom-call | flops 1000 | bytes 1000 | tf_op jit(solution)/shard_map/product_coded/pallas_call | solution.py:236
  37.0 5.0 %pack_left.3.left = bf16[432,2304]{1,0:T(8,128)(2,1)S(1)} custom-call(s32[8,16]{1,0:T(8,128)S(1)} %copy-done.7, bf16[8,138,16,138]{3,2,1,0:T(8,128)(2,1)} %bitcast.39, s16[3024,128]{1,0:T(8,128)(2,1)S(1)} %product_coded.6.after), custom_call_target="tpu_custom_call" | custom-call | flops 1000 | bytes 1000 | tf_op jit(solution)/shard_map/pack_left/pallas_call | solution.py:76
  43.2 2.1 %product_coded.10 = s16[1952,128]{1,0:T(8,128)(2,1)S(1)} custom-call(s32[2]{0:T(128)S(1)} %pad_add_fusion.others_0_.spot.place, bf16[432,2304]{1,0:T(8,128)(2,1)S(1)} %pack_left.3.left, bf16[16,2304,128]{2,1,0:T(8,128)(2,1)S(1)} %get-tuple-element.18.after.near, f32[432,256]{1,0:T(8,128)S(1)} %product_tails.3.tails.after, ...), custom_call_target="tpu_custom_call" | custom-call | flops 1000 | bytes 1000 | tf_op jit(solution)/shard_map/product_coded/pallas_call | solution.py:236
  49.4 3.7 %collective-permute-start.7 = (s16[1952,128]{1,0:T(8,128)(2,1)S(1)}, s16[1952,128]{1,0:T(8,128)(2,1)S(1)}, u32[]{:S(2)}, u32[]{:S(2)}) collective-permute-start(s16[1952,128]{1,0:T(8,128)(2,1)S(1)} %product_coded.11), channel_id=1, source_target_pairs={{0,2},{1,3},{2,0},{3,1},{4,6},{5,7},{6,4},{7,5},{8,10},{9,11},{10,... | collective-permute-start | bytes 1499144 | tf_op jit(solution)/shard_map/ppermute | solution.py:303
  56.4 2.3 %product_own.2.after.own = f32[3024,128]{1,0:T(8,128)S(1)} custom-call(s32[2]{0:T(128)S(1)} %pad_add_fusion.others_0_.spot.place, bf16[672,2304]{1,0:T(8,128)(2,1)S(1)} %pack_left.2.left, bf16[16,2304,128]{2,1,0:T(8,128)(2,1)S(1)} %get-tuple-element.18.after.near, f32[672,256]{1,0:T(8,128)S(1)} %product_tails.2.tails.after, ...), custom_call_target="tpu_custom_call" | custom-call | flops 1000 | bytes 1000 | tf_op jit(solution)/shard_map/product_own/pallas_call | solution.py:236
  60.5 5.2 %fetch.1 = (bf16[56,8,16384]{2,1,0:T(8,128)(2,1)S(1)}, f32[8,128]{1,0:T(8,128)S(1)}) custom-call(bf16[138,8,16384]{2,1,0:T(8,128)(2,1)} %bitcast.35, f32[1952,128]{1,0:T(8,128)S(1)} %product_own.3.after.own), custom_call_target="tpu_custom_call" | custom-call | flops 1000 | bytes 1000 | tf_op jit(solution)/shard_map/fetch/pallas_call | solution.py:343
  65.9 2.1 %merge.2 = (f32[768,128]{1,0:T(8,128)S(1)}, s16[768,128]{1,0:T(8,128)(2,1)S(1)}, s16[768,128]{1,0:T(8,128)(2,1)S(1)}, s16[768,128]{1,0:T(8,128)(2,1)S(1)}) custom-call(s32[2]{0:T(128)S(1)} %pad_add_fusion.others_0_.spot.place, f32[3024,128]{1,0:T(8,128)S(1)} %product_own.2.after.own, s16[3024,128]{1,0:T(8,128)(2,1)S(1)} %collective-permute-done.in1, ...), custom_call_target="tpu_custom_call" | custom-call | flops 1000 | bytes 1000 | tf_op jit(solution)/shard_map/merge/pallas_call | solution.py:286
  68.0 3.9 %collective-permute-start.3 = (s16[768,128]{1,0:T(8,128)(2,1)S(1)}, s16[768,128]{1,0:T(8,128)(2,1)S(1)}, u32[]{:S(2)}, u32[]{:S(2)}) collective-permute-start(s16[768,128]{1,0:T(8,128)(2,1)S(1)} %get-tuple-element.22), channel_id=1, source_target_pairs={{0,2},{1,3},{2,0},{3,1},{4,6},{5,7},{6,4},{7,5},{8,10},{9,11},{10,... | collective-permute-start | bytes 589832 | tf_op jit(solution)/shard_map/ppermute | solution.py:303
  73.0 2.2 %collective-permute-start.5 = (s16[768,128]{1,0:T(8,128)(2,1)S(1)}, s16[768,128]{1,0:T(8,128)(2,1)S(1)}, u32[]{:S(2)}, u32[]{:S(2)}) collective-permute-start(s16[768,128]{1,0:T(8,128)(2,1)S(1)} %get-tuple-element.24), channel_id=1, source_target_pairs={{0,3},{1,0},{2,1},{3,2},{4,7},{5,4},{6,5},{7,6},{8,11},{9,8},{10,9... | collective-permute-start | bytes 589832 | tf_op jit(solution)/shard_map/ppermute | solution.py:303
  76.7 8.1 %collective-permute-start.9 = (s16[496,128]{1,0:T(8,128)(2,1)S(1)}, s16[496,128]{1,0:T(8,128)(2,1)S(1)}, u32[]{:S(2)}, u32[]{:S(2)}) collective-permute-start(s16[496,128]{1,0:T(8,128)(2,1)S(1)} %get-tuple-element.28), channel_id=1, source_target_pairs={{0,8},{1,9},{2,10},{3,11},{4,12},{5,13},{6,14},{7,15},{8,0},{9,1},... | collective-permute-start | bytes 380936 | tf_op jit(solution)/shard_map/ppermute | solution.py:303
  84.8 3.2 %collective-permute-start.11 = (s16[496,128]{1,0:T(8,128)(2,1)S(1)}, s16[496,128]{1,0:T(8,128)(2,1)S(1)}, u32[]{:S(2)}, u32[]{:S(2)}) collective-permute-start(s16[496,128]{1,0:T(8,128)(2,1)S(1)} %get-tuple-element.30), channel_id=1, source_target_pairs={{0,12},{1,13},{2,14},{3,15},{4,0},{5,1},{6,2},{7,3},{8,4},{9,5},{1... | collective-permute-start | bytes 380936 | tf_op jit(solution)/shard_map/ppermute | solution.py:303
  88.1 9.6 %collocate.2 = (bf16[84,8,138]{2,1,0:T(8,128)(2,1)S(1)}, f32[16,8,1024]{2,1,0:T(8,128)S(1)}) custom-call(s32[2]{0:T(128)S(1)} %pad_add_fusion.others_0_.spot.place, s32[8]{0:T(128)S(1)} %bitcast.31, s32[8]{0:T(128)S(1)} %bitcast.33, f32[768,128]{1,0:T(8,128)S(1)} %get-tuple-element.21.after.own, s16[768,128]{1,0:T(8,128)(2,1)S(1)} %collective-permute-done.3.in1, ...), custom_call_target="tpu_custom_call" | custom-call | flops 1000 | bytes 1000 | tf_op jit(solution)/shard_map/collocate/pallas_call | solution.py:441
  97.8 8.8 %collocate.3 = (bf16[54,8,138]{2,1,0:T(8,128)(2,1)S(1)}, f32[16,8,1152]{2,1,0:T(8,128)}) custom-call(s32[2]{0:T(128)S(1)} %pad_add_fusion.others_0_.spot.place, s32[8]{0:T(128)S(1)} %bitcast.32, s32[8]{0:T(128)S(1)} %bitcast.34, f32[496,128]{1,0:T(8,128)S(1)} %get-tuple-element.25.after.own, s16[496,128]{1,0:T(8,128)(2,1)S(1)} %collective-permute-done.9.in1, ...), custom_call_target="tpu_custom_call" | custom-call | flops 1000 | bytes 1000 | tf_op jit(solution)/shard_map/collocate/pallas_call | solution.py:441
  106.7 3.6 %all-to-all-start = ((f32[16,8,1152]{2,1,0:T(8,128)}), f32[16,8,1152]{2,1,0:T(8,128)S(1)}, u32[]{:S(2)}, u32[]{:S(2)}) async-start(f32[16,8,1152]{2,1,0:T(8,128)} %get-tuple-element.33), calls=%async_computation | async-start | bytes 1179648 | tf_op jit(solution)/shard_map/all_to_all | solution.py:561
  110.3 10.4 %all-to-all-done.points = f32[16,8,1152]{2,1,0:T(8,128)S(1)} async-done(((f32[16,8,1152]{2,1,0:T(8,128)}), f32[16,8,1152]{2,1,0:T(8,128)S(1)}, u32[]{:S(2)}, u32[]{:S(2)}) %all-to-all-start) | async-done | bytes 589856 | tf_op jit(solution)/shard_map/all_to_all | solution.py:561
  124.6 2.7 %collective-permute-start.14 = (f32[16,1024]{1,0:T(8,128)S(1)}, f32[16,1024]{1,0:T(8,128)S(1)}, u32[]{:S(2)}, u32[]{:S(2)}) collective-permute-start(f32[16,1024]{1,0:T(8,128)S(1)} %get-tuple-element.35), channel_id=1, source_target_pairs={{0,64},{16,80},{32,96},{48,112},{64,0},{80,16},{96,32},{112,48},{1... | collective-permute-start | bytes 196616 | tf_op jit(solution)/shard_map/ppermute | solution.py:538
  128.8 2.1 %collective-permute-done.14.in2 = f32[16,1024]{1,0:T(8,128)S(1)} collective-permute-done((f32[16,1024]{1,0:T(8,128)S(1)}, f32[16,1024]{1,0:T(8,128)S(1)}, u32[]{:S(2)}, u32[]{:S(2)}) %collective-permute-start.14) | collective-permute-done | bytes 65568 | tf_op jit(solution)/shard_map/ppermute | solution.py:538
  133.6 3.5 %all-to-all-start.1 = ((f32[16,8,128]{2,1,0:T(8,128)}), f32[16,8,128]{2,1,0:T(8,128)S(1)}, u32[]{:S(2)}, u32[]{:S(2)}) async-start(f32[16,8,128]{2,1,0:T(8,128)} %filter_rows.1), calls=%async_computation.1 | async-start | bytes 131072 | tf_op jit(solution)/shard_map/all_to_all | solution.py:564
  138.0 6.7 %all-to-all-done.1 = f32[16,8,128]{2,1,0:T(8,128)S(1)} async-done(((f32[16,8,128]{2,1,0:T(8,128)}), f32[16,8,128]{2,1,0:T(8,128)S(1)}, u32[]{:S(2)}, u32[]{:S(2)}) %all-to-all-start.1) | async-done | bytes 65568 | tf_op jit(solution)/shard_map/all_to_all | solution.py:564
  (60 shorter events, 28.0 us)
Async XLA Ops:
  25.3 29.8 %collective-permute-start = (s16[3024,128]{1,0:T(8,128)(2,1)S(1)}, s16[3024,128]{1,0:T(8,128)(2,1)S(1)}, u32[]{:S(2)}, u32[]{:S(2)}) collective-permute-start(s16[3024,128]{1,0:T(8,128)(2,1)S(1)} %product_coded.8), channel_id=1, source_target_pairs={{0,4},{1,5},{2,6},{3,7},{4,8},{5,9},{6,10},{7,11},{8,12},{9,13},{1... | collective-permute-start | bytes 2322440 | tf_op jit(solution)/shard_map/ppermute | solution.py:303
  29.8 35.8 %collective-permute-start.1 = (s16[3024,128]{1,0:T(8,128)(2,1)S(1)}, s16[3024,128]{1,0:T(8,128)(2,1)S(1)}, u32[]{:S(2)}, u32[]{:S(2)}) collective-permute-start(s16[3024,128]{1,0:T(8,128)(2,1)S(1)} %product_coded.9), channel_id=1, source_target_pairs={{0,8},{1,9},{2,10},{3,11},{4,12},{5,13},{6,14},{7,15},{8,0},{9,1},... | collective-permute-start | bytes 2322440 | tf_op jit(solution)/shard_map/ppermute | solution.py:303
  35.6 30.3 %collective-permute-start.2 = (s16[3024,128]{1,0:T(8,128)(2,1)S(1)}, s16[3024,128]{1,0:T(8,128)(2,1)S(1)}, u32[]{:S(2)}, u32[]{:S(2)}) collective-permute-start(s16[3024,128]{1,0:T(8,128)(2,1)S(1)} %product_coded.6.after), channel_id=1, source_target_pairs={{0,12},{1,13},{2,14},{3,15},{4,0},{5,1},{6,2},{7,3},{8,4},{9,5},{1... | collective-permute-start | bytes 2322440 | tf_op jit(solution)/shard_map/ppermute | solution.py:303
  45.3 27.6 %collective-permute-start.6 = (s16[1952,128]{1,0:T(8,128)(2,1)S(1)}, s16[1952,128]{1,0:T(8,128)(2,1)S(1)}, u32[]{:S(2)}, u32[]{:S(2)}) collective-permute-start(s16[1952,128]{1,0:T(8,128)(2,1)S(1)} %product_coded.10), channel_id=1, source_target_pairs={{0,1},{1,2},{2,3},{3,0},{4,5},{5,6},{6,7},{7,4},{8,9},{9,10},{10,1... | collective-permute-start | bytes 1499144 | tf_op jit(solution)/shard_map/ppermute | solution.py:303
  49.4 25.8 %collective-permute-start.7 = (s16[1952,128]{1,0:T(8,128)(2,1)S(1)}, s16[1952,128]{1,0:T(8,128)(2,1)S(1)}, u32[]{:S(2)}, u32[]{:S(2)}) collective-permute-start(s16[1952,128]{1,0:T(8,128)(2,1)S(1)} %product_coded.11), channel_id=1, source_target_pairs={{0,2},{1,3},{2,0},{3,1},{4,6},{5,7},{6,4},{7,5},{8,10},{9,11},{10,... | collective-permute-start | bytes 1499144 | tf_op jit(solution)/shard_map/ppermute | solution.py:303
  55.1 20.1 %collective-permute-start.8 = (s16[1952,128]{1,0:T(8,128)(2,1)S(1)}, s16[1952,128]{1,0:T(8,128)(2,1)S(1)}, u32[]{:S(2)}, u32[]{:S(2)}) collective-permute-start(s16[1952,128]{1,0:T(8,128)(2,1)S(1)} %product_coded.7.after), channel_id=1, source_target_pairs={{0,3},{1,0},{2,1},{3,2},{4,7},{5,4},{6,5},{7,6},{8,11},{9,8},{10,9... | collective-permute-start | bytes 1499144 | tf_op jit(solution)/shard_map/ppermute | solution.py:303
  68.0 16.8 %collective-permute-start.3 = (s16[768,128]{1,0:T(8,128)(2,1)S(1)}, s16[768,128]{1,0:T(8,128)(2,1)S(1)}, u32[]{:S(2)}, u32[]{:S(2)}) collective-permute-start(s16[768,128]{1,0:T(8,128)(2,1)S(1)} %get-tuple-element.22), channel_id=1, source_target_pairs={{0,2},{1,3},{2,0},{3,1},{4,6},{5,7},{6,4},{7,5},{8,10},{9,11},{10,... | collective-permute-start | bytes 589832 | tf_op jit(solution)/shard_map/ppermute | solution.py:303
  71.9 16.1 %collective-permute-start.4 = (s16[768,128]{1,0:T(8,128)(2,1)S(1)}, s16[768,128]{1,0:T(8,128)(2,1)S(1)}, u32[]{:S(2)}, u32[]{:S(2)}) collective-permute-start(s16[768,128]{1,0:T(8,128)(2,1)S(1)} %get-tuple-element.23), channel_id=1, source_target_pairs={{0,1},{1,2},{2,3},{3,0},{4,5},{5,6},{6,7},{7,4},{8,9},{9,10},{10,1... | collective-permute-start | bytes 589832 | tf_op jit(solution)/shard_map/ppermute | solution.py:303
  73.0 15.1 %collective-permute-start.5 = (s16[768,128]{1,0:T(8,128)(2,1)S(1)}, s16[768,128]{1,0:T(8,128)(2,1)S(1)}, u32[]{:S(2)}, u32[]{:S(2)}) collective-permute-start(s16[768,128]{1,0:T(8,128)(2,1)S(1)} %get-tuple-element.24), channel_id=1, source_target_pairs={{0,3},{1,0},{2,1},{3,2},{4,7},{5,4},{6,5},{7,6},{8,11},{9,8},{10,9... | collective-permute-start | bytes 589832 | tf_op jit(solution)/shard_map/ppermute | solution.py:303
  76.7 21.0 %collective-permute-start.9 = (s16[496,128]{1,0:T(8,128)(2,1)S(1)}, s16[496,128]{1,0:T(8,128)(2,1)S(1)}, u32[]{:S(2)}, u32[]{:S(2)}) collective-permute-start(s16[496,128]{1,0:T(8,128)(2,1)S(1)} %get-tuple-element.28), channel_id=1, source_target_pairs={{0,8},{1,9},{2,10},{3,11},{4,12},{5,13},{6,14},{7,15},{8,0},{9,1},... | collective-permute-start | bytes 380936 | tf_op jit(solution)/shard_map/ppermute | solution.py:303
  84.8 12.9 %collective-permute-start.10 = (s16[496,128]{1,0:T(8,128)(2,1)S(1)}, s16[496,128]{1,0:T(8,128)(2,1)S(1)}, u32[]{:S(2)}, u32[]{:S(2)}) collective-permute-start(s16[496,128]{1,0:T(8,128)(2,1)S(1)} %get-tuple-element.29), channel_id=1, source_target_pairs={{0,4},{1,5},{2,6},{3,7},{4,8},{5,9},{6,10},{7,11},{8,12},{9,13},{1... | collective-permute-start | bytes 380936 | tf_op jit(solution)/shard_map/ppermute | solution.py:303
  84.8 12.9 %collective-permute-start.11 = (s16[496,128]{1,0:T(8,128)(2,1)S(1)}, s16[496,128]{1,0:T(8,128)(2,1)S(1)}, u32[]{:S(2)}, u32[]{:S(2)}) collective-permute-start(s16[496,128]{1,0:T(8,128)(2,1)S(1)} %get-tuple-element.30), channel_id=1, source_target_pairs={{0,12},{1,13},{2,14},{3,15},{4,0},{5,1},{6,2},{7,3},{8,4},{9,5},{1... | collective-permute-start | bytes 380936 | tf_op jit(solution)/shard_map/ppermute | solution.py:303
  97.8 33.9 %copy-start.1 = (f32[256,256]{1,0:T(8,128)S(1)}, f32[256,256]{1,0:T(8,128)}, u32[]{:S(2)}) copy-start(f32[256,256]{1,0:T(8,128)} %constant.98.clone.second) | copy-start | bytes 786436
  97.8 33.8 %copy-start.2 = (f32[256,256]{1,0:T(8,128)S(1)}, f32[256,256]{1,0:T(8,128)}, u32[]{:S(2)}) copy-start(f32[256,256]{1,0:T(8,128)} %constant.99.clone.third) | copy-start | bytes 786436
  97.8 33.8 %copy-start.3 = (f32[256,128]{1,0:T(8,128)S(1)}, f32[256,128]{1,0:T(8,128)}, u32[]{:S(2)}) copy-start(f32[256,128]{1,0:T(8,128)} %constant.97.clone.first) | copy-start | bytes 393220
  97.8 33.8 %copy-start.4 = (f32[128,256]{1,0:T(8,128)S(1)}, f32[128,256]{1,0:T(8,128)}, u32[]{:S(2)}) copy-start(f32[128,256]{1,0:T(8,128)} %constant.100.clone.last) | copy-start | bytes 393220
  97.8 33.8 %copy-start.5 = (f32[128,128]{1,0:T(8,128)S(1)}, f32[128,128]{1,0:T(8,128)}, u32[]{:S(2)}) copy-start(f32[128,128]{1,0:T(8,128)} %constant.101.clone.tc) | copy-start | bytes 196612
  97.8 33.8 %copy-start.6 = (f32[128,128]{1,0:T(8,128)S(1)}, f32[128,128]{1,0:T(8,128)}, u32[]{:S(2)}) copy-start(f32[128,128]{1,0:T(8,128)} %constant.102.clone.ts) | copy-start | bytes 196612
  106.7 14.1 %all-to-all-start = ((f32[16,8,1152]{2,1,0:T(8,128)}), f32[16,8,1152]{2,1,0:T(8,128)S(1)}, u32[]{:S(2)}, u32[]{:S(2)}) async-start(f32[16,8,1152]{2,1,0:T(8,128)} %get-tuple-element.33), calls=%async_computation | async-start | bytes 1179648 | tf_op jit(solution)/shard_map/all_to_all | solution.py:561
  121.4 1.6 %collective-permute-start.12 = (f32[4,16,1024]{2,1,0:T(8,128)S(1)}, f32[4,16,1024]{2,1,0:T(8,128)S(1)}, u32[]{:S(2)}, u32[]{:S(2)}) collective-permute-start(f32[4,16,1024]{2,1,0:T(8,128)S(1)} %dynamic-slice_bitcast_fusion), channel_id=1, source_target_pairs={{0,16},{16,0},{32,48},{48,32},{64,80},{80,64},{96,112},{112,96},{1... | collective-permute-start | bytes 786440 | tf_op jit(solution)/shard_map/ppermute | solution.py:534
  123.1 5.7 %collective-permute-start.13 = (f32[16,1024]{1,0:T(8,128)S(1)}, f32[16,1024]{1,0:T(8,128)S(1)}, u32[]{:S(2)}, u32[]{:S(2)}) collective-permute-start(f32[16,1024]{1,0:T(8,128)S(1)} %get-tuple-element.36), channel_id=1, source_target_pairs={{0,32},{16,48},{32,64},{48,80},{64,96},{80,112},{96,0},{112,16},{1... | collective-permute-start | bytes 196616 | tf_op jit(solution)/shard_map/ppermute | solution.py:538
  124.6 6.2 %collective-permute-start.14 = (f32[16,1024]{1,0:T(8,128)S(1)}, f32[16,1024]{1,0:T(8,128)S(1)}, u32[]{:S(2)}, u32[]{:S(2)}) collective-permute-start(f32[16,1024]{1,0:T(8,128)S(1)} %get-tuple-element.35), channel_id=1, source_target_pairs={{0,64},{16,80},{32,96},{48,112},{64,0},{80,16},{96,32},{112,48},{1... | collective-permute-start | bytes 196616 | tf_op jit(solution)/shard_map/ppermute | solution.py:538
  127.4 4.3 %collective-permute-start.15 = (f32[16,1024]{1,0:T(8,128)S(1)}, f32[16,1024]{1,0:T(8,128)S(1)}, u32[]{:S(2)}, u32[]{:S(2)}) collective-permute-start(f32[16,1024]{1,0:T(8,128)S(1)} %get-tuple-element.34), channel_id=1, source_target_pairs={{0,96},{16,112},{32,0},{48,16},{64,32},{80,48},{96,64},{112,80},{1... | collective-permute-start | bytes 196616 | tf_op jit(solution)/shard_map/ppermute | solution.py:538
  133.6 11.1 %all-to-all-start.1 = ((f32[16,8,128]{2,1,0:T(8,128)}), f32[16,8,128]{2,1,0:T(8,128)S(1)}, u32[]{:S(2)}, u32[]{:S(2)}) async-start(f32[16,8,128]{2,1,0:T(8,128)} %filter_rows.1), calls=%async_computation.1 | async-start | bytes 131072 | tf_op jit(solution)/shard_map/all_to_all | solution.py:564
  (4 other events, 74.9 us)

commit v2 on v1

--- a/solution.py
+++ b/solution.py
@@ -23,7 +23,6 @@
 FOLD = (96, 64)
 STEP = (28, 18)
 POINTS = 2048
-EARLY = 56
 
 
 def in_hbm(array):
@@ -303,7 +302,7 @@
     return lax.ppermute(array, "col", turn(d, 0) if axis == 0 else turn(0, d))
 
 
-def exchange_products(spot, blocks_a, pattern, blocks_b, by_point, before):
+def exchange_products(spot, blocks_a, pattern, blocks_b, before):
     blocks_a = jnp.transpose(blocks_a, (0, 2, 1, 3))
     near, rest = pack_right(jnp.transpose(blocks_b, (0, 2, 1, 3)), [spot] + before)
     after = near
@@ -322,41 +321,18 @@
         after = product_group(half, 0, spot, *lefts[half], after)
         owns.append(after)
 
-    early, after = fetch(by_point, after)
-
     def finish(half, after):
         mine, *outs = merge(half, spot, owns[half], parts[half], after)
         return mine, [send(outs[d - 1], 1 - half, d) for d in (2, 1, 3)]
 
-    return finish, early, after
-
-
-def fetch_kernel(rows, after, out, done, sem):
-    copy = pltpu.make_async_copy(rows.at[pl.ds(0, EARLY)], out, sem)
-    copy.start()
-    done[...] = jnp.zeros((8, 128), F32)
-    copy.wait()
-
-
-def fetch(rows, after):
-    vmem = pl.BlockSpec(memory_space=pltpu.VMEM)
-    return pl.pallas_call(
-        fetch_kernel,
-        in_specs=[pl.BlockSpec(memory_space=pltpu.HBM), pl.BlockSpec(memory_space=pl.ANY)],
-        out_specs=[vmem, vmem],
-        out_shape=[pltpu.VMEM((EARLY, 8, 16384), BF16), jax.ShapeDtypeStruct((8, 128), F32)],
-        scratch_shapes=[pltpu.SemaphoreType.DMA],
-        compiler_params=pltpu.CompilerParams(vmem_limit_bytes=20 * MIB),
-        cost_estimate=pl.CostEstimate(flops=1000, bytes_accessed=1000, transcendentals=0),
-        name="fetch",
-    )(in_hbm(rows), after)
+    return finish, after
 
 
 def collocate_kernel(half, spot, keep, ids, own, in1, in2, in3, cols, rows, after, *rest):
     size = FOLD[half]
-    before, density, out, stacked, right, held, held_cols, sems = rest
+    before = rest[0] if half else None
+    density, out, stacked, right, held, held_cols, sems = rest[half:]
     count = ROWS[half]
-    first = EARLY if half == 0 else 0
     tiles = 16384 // POINTS
 
     def copies(g):
@@ -364,7 +340,7 @@
         return (
             pltpu.make_async_copy(cols.at[0, :, span], held_cols.at[g], sems.at[0, g]),
             pltpu.make_async_copy(
-                rows.at[pl.ds(CUT[half] // 8 + first, count // 8 - first), :, span], held.at[g], sems.at[1, g]
+                rows.at[pl.ds(CUT[half] // 8, count // 8), :, span], held.at[g], sems.at[1, g]
             ),
         )
 
@@ -412,10 +388,7 @@
         for t in range(POINTS // 256):
             here = slice(t * 256, (t + 1) * 256)
             inner = jnp.dot(stacked[...], right[:, here], preferred_element_type=F32).reshape(count // 8, 8, 256)
-            total = jnp.sum(inner[first:] * held[g, :, :, here].astype(F32), axis=0)
-            if half == 0:
-                at = pl.ds(pl.multiple_of(g * POINTS + t * 256, 256), 256)
-                total = total + jnp.sum(inner[:first] * before[:, :, at].astype(F32), axis=0)
+            total = jnp.sum(inner * held[g, :, :, here].astype(F32), axis=0)
             within = slice(t % 4 * 256, t % 4 * 256 + 256)
             if half == 1:
                 total = total + before[per * g + t // 4, :, within]
@@ -436,7 +409,6 @@
     count = ROWS[half]
     wide = 1152 if half else 1024
     vmem = pl.BlockSpec(memory_space=pltpu.VMEM)
-    first = EARLY if half == 0 else 0
     tiles = 16384 // POINTS
     return pl.pallas_call(
         functools.partial(collocate_kernel, half),
@@ -444,12 +416,12 @@
         + [vmem] * 4
         + [pl.BlockSpec(memory_space=pltpu.HBM)] * 2
         + [pl.BlockSpec(memory_space=pl.ANY)]
-        + [vmem],
+        + [vmem] * half,
         out_specs=[vmem] * 2,
         scratch_shapes=[
             pltpu.VMEM((count, 256), BF16),
             pltpu.VMEM((256, POINTS), BF16),
-            pltpu.VMEM((tiles, count // 8 - first, 8, POINTS), BF16),
+            pltpu.VMEM((tiles, count // 8, 8, POINTS), BF16),
             pltpu.VMEM((tiles, BS, POINTS), BF16),
             pltpu.SemaphoreType.DMA((2, tiles)),
         ],
@@ -457,7 +429,7 @@
             jax.ShapeDtypeStruct((count // 8, 8, BS), BF16),
             jax.ShapeDtypeStruct((16, 8, wide), F32),
         ],
-        compiler_params=pltpu.CompilerParams(vmem_limit_bytes=(24, 28)[half] * MIB),
+        compiler_params=pltpu.CompilerParams(vmem_limit_bytes=(38, 28)[half] * MIB),
         cost_estimate=pl.CostEstimate(flops=1000, bytes_accessed=1000, transcendentals=0),
         name="collocate",
     )(spot, keep, ids, own, *parts, in_hbm(basis_cols), in_hbm(basis_rows), after, *before)
@@ -545,7 +517,7 @@
     spot = jnp.stack([place // 4, place % 4])
     keep, ids = filter_mask.reshape(8), task_brick.reshape(8)
     by_point = jnp.transpose(basis_rows, (1, 0, 2))
-    finish, early, after = exchange_products(spot, blocks_a, pattern_a, blocks_b, by_point, [kern])
+    finish, after = exchange_products(spot, blocks_a, pattern_a, blocks_b, [kern])
     densities, before, sums = [], [], []
     for half in range(2):
         sums.append(finish(half, after))
@@ -553,7 +525,7 @@
     for half in range(2):
         own, parts = sums[half]
         density, after = collocate(
-            half, spot, keep, ids, own, parts, basis_cols, by_point, [early] if half == 0 else before, after
+            half, spot, keep, ids, own, parts, basis_cols, by_point, before, after
         )
         densities.append(density)
         before = [after]

time: 146 us -> 142 us (0.973)
  Pallas kernels: 75.2 us -> 71.1 us
  waiting for transfers between devices: 21.6 us -> 25.6 us
  starting transfers between devices: 44.5 us -> 41.2 us
    ppermute x12, starting transfers between devices: 31.5 us -> 25.2 us  [send(): return lax.ppermute(array, 'col', turn(d, 0) if axis == 0 else turn(0, d))]
    pallas_call x1 -> x0, Pallas kernels: 5.19 us -> none  [fetch(): pl.pallas_call(fetch_kernel, in_specs=[pl.BlockSpec(memory_space=pltpu.HB...]
    ppermute x12, waiting for transfers between devices: 0.21 us -> 3.99 us  [send(): return lax.ppermute(array, 'col', turn(d, 0) if axis == 0 else turn(0, d))]
    all_to_all x1, starting transfers between devices: 3.63 us -> 6.62 us  [shards(): lax.all_to_all(points, 'col', split_axis=0, concat_axis=0, tiled=True)]
  transfers between devices with their start and end apart: 18 -> 18, of which waited for: 6 -> 11; matrix products, arithmetic and copies ran while one was open for 1% -> 1% of each run, Pallas kernels for 28% -> 26%
where the time goes in v2:
time: 142 us
  Pallas kernels  71.1 us (50%)
  starting transfers between devices  41.2 us (29%)
  waiting for transfers between devices  25.6 us (18%)
  local copies, waits for them, and re-layouts  1.95 us (1%)
    ppermute x12, starting transfers between devices, send(): return lax.ppermute(array, 'col', turn(d, 0) if axis == 0 else turn(0, d))  25.2 us
    pallas_call x2, Pallas kernels, collocate(): pl.pallas_call(functools.partial(collocate_kernel, half), in_specs=[pl.Bl...  19.5 us
    pallas_call x8, Pallas kernels, product_group(): pl.pallas_call(functools.partial(product_kernel, half, d), in_specs=[pl.B...  18.6 us
    pallas_call x1, Pallas kernels, pack_right(): pl.pallas_call(pack_right_kernel, grid=(8,), in_specs=[pl.BlockSpec((2, B...  12.5 us
    pallas_call x2, Pallas kernels, pack_left(): pl.pallas_call(functools.partial(pack_left_kernel, count // 2), grid=(ROW...  12 us
    all_to_all x1, waiting for transfers between devices, shards(): lax.all_to_all(points, 'col', split_axis=0, concat_axis=0, tiled=True)  10.6 us
    all_to_all x1, waiting for transfers between devices, shards(): lax.all_to_all(filtered, 'col', split_axis=0, concat_axis=0, tiled=True)  6.71 us
    all_to_all x1, starting transfers between devices, shards(): lax.all_to_all(points, 'col', split_axis=0, concat_axis=0, tiled=True)  6.62 us
  transfers between devices with their start and end apart: 18, of which 11 were waited for; matrix products, arithmetic and copies ran while one was open for 1% of the time, Pallas kernels for 26%

profile of v2, /device:TPU:0, one launch (start us, length us, event | category | flops | bytes accessed | tf_op | source)
XLA Modules:
  0.0 141.9 jit_solution(7319584268489171936)
XLA Ops:
  1.9 12.5 %pack_right.1 = (bf16[16,2304,128]{2,1,0:T(8,128)(2,1)S(1)}, bf16[2304,256]{1,0:T(8,128)(2,1)S(1)}) custom-call(bf16[16,138,16,138]{3,2,1,0:T(8,128)(2,1)} %bitcast.39, s32[2]{0:T(128)S(1)} %pad_add_fusion.others_0_.spot.place, f32[128,128]{1,0:T(8,128)S(1)} %bitcast.29), custom_call_target="tpu_custom_call" | custom-call | flops 1000 | bytes 1000 | tf_op jit(solution)/shard_map/pack_right/pallas_call | solution.py:121
  14.5 7.0 %pack_left.2.left = bf16[672,2304]{1,0:T(8,128)(2,1)S(1)} custom-call(s32[8,16]{1,0:T(8,128)S(1)} %copy-done.7, bf16[8,138,16,138]{3,2,1,0:T(8,128)(2,1)} %bitcast.37, bf16[16,2304,128]{2,1,0:T(8,128)(2,1)S(1)} %get-tuple-element.16.after.near), custom_call_target="tpu_custom_call" | custom-call | flops 1000 | bytes 1000 | tf_op jit(solution)/shard_map/pack_left/pallas_call | solution.py:75
  22.5 2.8 %product_coded.9 = s16[3024,128]{1,0:T(8,128)(2,1)S(1)} custom-call(s32[2]{0:T(128)S(1)} %pad_add_fusion.others_0_.spot.place, bf16[672,2304]{1,0:T(8,128)(2,1)S(1)} %pack_left.2.left, bf16[16,2304,128]{2,1,0:T(8,128)(2,1)S(1)} %get-tuple-element.16.after.near, f32[672,256]{1,0:T(8,128)S(1)} %product_tails.2.tails.after, f32[672,256]{1,0:T(8,128)S(1)} %product_tails.2.tails.after), custom_call_target="tpu_custom_call" | custom-call | flops 1000 | bytes 1000 | tf_op jit(solution)/shard_map/product_coded/pallas_call | solution.py:235
  25.3 3.4 %collective-permute-start.1 = (s16[3024,128]{1,0:T(8,128)(2,1)S(1)}, s16[3024,128]{1,0:T(8,128)(2,1)S(1)}, u32[]{:S(2)}, u32[]{:S(2)}) collective-permute-start(s16[3024,128]{1,0:T(8,128)(2,1)S(1)} %product_coded.9), channel_id=1, source_target_pairs={{0,8},{1,9},{2,10},{3,11},{4,12},{5,13},{6,14},{7,15},{8,0},{9,1},... | collective-permute-start | bytes 2322440 | tf_op jit(solution)/shard_map/ppermute | solution.py:302
  28.7 2.8 %product_coded.8 = s16[3024,128]{1,0:T(8,128)(2,1)S(1)} custom-call(s32[2]{0:T(128)S(1)} %pad_add_fusion.others_0_.spot.place, bf16[672,2304]{1,0:T(8,128)(2,1)S(1)} %pack_left.2.left, bf16[16,2304,128]{2,1,0:T(8,128)(2,1)S(1)} %get-tuple-element.16.after.near, f32[672,256]{1,0:T(8,128)S(1)} %product_tails.2.tails.after, f32[672,256]{1,0:T(8,128)S(1)} %product_tails.2.tails.after), custom_call_target="tpu_custom_call" | custom-call | flops 1000 | bytes 1000 | tf_op jit(solution)/shard_map/product_coded/pallas_call | solution.py:235
  32.2 2.8 %product_coded.6.after = s16[3024,128]{1,0:T(8,128)(2,1)S(1)} custom-call(s32[2]{0:T(128)S(1)} %pad_add_fusion.others_0_.spot.place, bf16[672,2304]{1,0:T(8,128)(2,1)S(1)} %pack_left.2.left, bf16[16,2304,128]{2,1,0:T(8,128)(2,1)S(1)} %get-tuple-element.16.after.near, f32[672,256]{1,0:T(8,128)S(1)} %product_tails.2.tails.after, ...), custom_call_target="tpu_custom_call" | custom-call | flops 1000 | bytes 1000 | tf_op jit(solution)/shard_map/product_coded/pallas_call | solution.py:235
  35.0 2.6 %collective-permute-start.2 = (s16[3024,128]{1,0:T(8,128)(2,1)S(1)}, s16[3024,128]{1,0:T(8,128)(2,1)S(1)}, u32[]{:S(2)}, u32[]{:S(2)}) collective-permute-start(s16[3024,128]{1,0:T(8,128)(2,1)S(1)} %product_coded.6.after), channel_id=1, source_target_pairs={{0,12},{1,13},{2,14},{3,15},{4,0},{5,1},{6,2},{7,3},{8,4},{9,5},{1... | collective-permute-start | bytes 2322440 | tf_op jit(solution)/shard_map/ppermute | solution.py:302
  37.6 5.0 %pack_left.3.left = bf16[432,2304]{1,0:T(8,128)(2,1)S(1)} custom-call(s32[8,16]{1,0:T(8,128)S(1)} %copy-done.7, bf16[8,138,16,138]{3,2,1,0:T(8,128)(2,1)} %bitcast.38, s16[3024,128]{1,0:T(8,128)(2,1)S(1)} %product_coded.6.after), custom_call_target="tpu_custom_call" | custom-call | flops 1000 | bytes 1000 | tf_op jit(solution)/shard_map/pack_left/pallas_call | solution.py:75
  43.8 2.1 %product_coded.11 = s16[1952,128]{1,0:T(8,128)(2,1)S(1)} custom-call(s32[2]{0:T(128)S(1)} %pad_add_fusion.others_0_.spot.place, bf16[432,2304]{1,0:T(8,128)(2,1)S(1)} %pack_left.3.left, bf16[16,2304,128]{2,1,0:T(8,128)(2,1)S(1)} %get-tuple-element.16.after.near, f32[432,256]{1,0:T(8,128)S(1)} %product_tails.3.tails.after, ...), custom_call_target="tpu_custom_call" | custom-call | flops 1000 | bytes 1000 | tf_op jit(solution)/shard_map/product_coded/pallas_call | solution.py:235
  45.9 4.0 %collective-permute-start.7 = (s16[1952,128]{1,0:T(8,128)(2,1)S(1)}, s16[1952,128]{1,0:T(8,128)(2,1)S(1)}, u32[]{:S(2)}, u32[]{:S(2)}) collective-permute-start(s16[1952,128]{1,0:T(8,128)(2,1)S(1)} %product_coded.11), channel_id=1, source_target_pairs={{0,2},{1,3},{2,0},{3,1},{4,6},{5,7},{6,4},{7,5},{8,10},{9,11},{10,... | collective-permute-start | bytes 1499144 | tf_op jit(solution)/shard_map/ppermute | solution.py:302
  55.1 2.5 %collective-permute-start.8 = (s16[1952,128]{1,0:T(8,128)(2,1)S(1)}, s16[1952,128]{1,0:T(8,128)(2,1)S(1)}, u32[]{:S(2)}, u32[]{:S(2)}) collective-permute-start(s16[1952,128]{1,0:T(8,128)(2,1)S(1)} %product_coded.7.after), channel_id=1, source_target_pairs={{0,3},{1,0},{2,1},{3,2},{4,7},{5,4},{6,5},{7,6},{8,11},{9,8},{10,9... | collective-permute-start | bytes 1499144 | tf_op jit(solution)/shard_map/ppermute | solution.py:302
  57.6 2.3 %product_own.2.after.own = f32[3024,128]{1,0:T(8,128)S(1)} custom-call(s32[2]{0:T(128)S(1)} %pad_add_fusion.others_0_.spot.place, bf16[672,2304]{1,0:T(8,128)(2,1)S(1)} %pack_left.2.left, bf16[16,2304,128]{2,1,0:T(8,128)(2,1)S(1)} %get-tuple-element.16.after.near, f32[672,256]{1,0:T(8,128)S(1)} %product_tails.2.tails.after, ...), custom_call_target="tpu_custom_call" | custom-call | flops 1000 | bytes 1000 | tf_op jit(solution)/shard_map/product_own/pallas_call | solution.py:235
  63.0 2.1 %merge.2 = (f32[768,128]{1,0:T(8,128)S(1)}, s16[768,128]{1,0:T(8,128)(2,1)S(1)}, s16[768,128]{1,0:T(8,128)(2,1)S(1)}, s16[768,128]{1,0:T(8,128)(2,1)S(1)}) custom-call(s32[2]{0:T(128)S(1)} %pad_add_fusion.others_0_.spot.place, f32[3024,128]{1,0:T(8,128)S(1)} %product_own.2.after.own, s16[3024,128]{1,0:T(8,128)(2,1)S(1)} %collective-permute-done.in1, ...), custom_call_target="tpu_custom_call" | custom-call | flops 1000 | bytes 1000 | tf_op jit(solution)/shard_map/merge/pallas_call | solution.py:285
  65.1 3.9 %collective-permute-start.3 = (s16[768,128]{1,0:T(8,128)(2,1)S(1)}, s16[768,128]{1,0:T(8,128)(2,1)S(1)}, u32[]{:S(2)}, u32[]{:S(2)}) collective-permute-start(s16[768,128]{1,0:T(8,128)(2,1)S(1)} %get-tuple-element.19), channel_id=1, source_target_pairs={{0,2},{1,3},{2,0},{3,1},{4,6},{5,7},{6,4},{7,5},{8,10},{9,11},{10,... | collective-permute-start | bytes 589832 | tf_op jit(solution)/shard_map/ppermute | solution.py:302
  70.1 2.2 %collective-permute-start.5 = (s16[768,128]{1,0:T(8,128)(2,1)S(1)}, s16[768,128]{1,0:T(8,128)(2,1)S(1)}, u32[]{:S(2)}, u32[]{:S(2)}) collective-permute-start(s16[768,128]{1,0:T(8,128)(2,1)S(1)} %get-tuple-element.21), channel_id=1, source_target_pairs={{0,3},{1,0},{2,1},{3,2},{4,7},{5,4},{6,5},{7,6},{8,11},{9,8},{10,9... | collective-permute-start | bytes 589832 | tf_op jit(solution)/shard_map/ppermute | solution.py:302
  75.3 3.0 %collective-permute-start.11 = (s16[496,128]{1,0:T(8,128)(2,1)S(1)}, s16[496,128]{1,0:T(8,128)(2,1)S(1)}, u32[]{:S(2)}, u32[]{:S(2)}) collective-permute-start(s16[496,128]{1,0:T(8,128)(2,1)S(1)} %get-tuple-element.26), channel_id=1, source_target_pairs={{0,12},{1,13},{2,14},{3,15},{4,0},{5,1},{6,2},{7,3},{8,4},{9,5},{1... | collective-permute-start | bytes 380936 | tf_op jit(solution)/shard_map/ppermute | solution.py:302
  80.4 10.7 %collocate.2 = (bf16[84,8,138]{2,1,0:T(8,128)(2,1)S(1)}, f32[16,8,1024]{2,1,0:T(8,128)S(1)}) custom-call(s32[2]{0:T(128)S(1)} %pad_add_fusion.others_0_.spot.place, s32[8]{0:T(128)S(1)} %bitcast.31, s32[8]{0:T(128)S(1)} %bitcast.33, f32[768,128]{1,0:T(8,128)S(1)} %get-tuple-element.18.after.own, s16[768,128]{1,0:T(8,128)(2,1)S(1)} %collective-permute-done.3.in1, ...), custom_call_target="tpu_custom_call" | custom-call | flops 1000 | bytes 1000 | tf_op jit(solution)/shard_map/collocate/pallas_call | solution.py:413
  91.2 8.8 %collocate.3 = (bf16[54,8,138]{2,1,0:T(8,128)(2,1)S(1)}, f32[16,8,1152]{2,1,0:T(8,128)}) custom-call(s32[2]{0:T(128)S(1)} %pad_add_fusion.others_0_.spot.place, s32[8]{0:T(128)S(1)} %bitcast.32, s32[8]{0:T(128)S(1)} %bitcast.34, f32[496,128]{1,0:T(8,128)S(1)} %get-tuple-element.22.after.own, s16[496,128]{1,0:T(8,128)(2,1)S(1)} %collective-permute-done.9.in1, ...), custom_call_target="tpu_custom_call" | custom-call | flops 1000 | bytes 1000 | tf_op jit(solution)/shard_map/collocate/pallas_call | solution.py:413
  100.0 6.6 %all-to-all-start = ((f32[16,8,1152]{2,1,0:T(8,128)}), f32[16,8,1152]{2,1,0:T(8,128)S(1)}, u32[]{:S(2)}, u32[]{:S(2)}) async-start(f32[16,8,1152]{2,1,0:T(8,128)} %get-tuple-element.29), calls=%async_computation | async-start | bytes 1179648 | tf_op jit(solution)/shard_map/all_to_all | solution.py:533
  106.7 10.6 %all-to-all-done.points = f32[16,8,1152]{2,1,0:T(8,128)S(1)} async-done(((f32[16,8,1152]{2,1,0:T(8,128)}), f32[16,8,1152]{2,1,0:T(8,128)S(1)}, u32[]{:S(2)}, u32[]{:S(2)}) %all-to-all-start) | async-done | bytes 589856 | tf_op jit(solution)/shard_map/all_to_all | solution.py:533
  121.2 2.7 %collective-permute-start.14 = (f32[16,1024]{1,0:T(8,128)S(1)}, f32[16,1024]{1,0:T(8,128)S(1)}, u32[]{:S(2)}, u32[]{:S(2)}) collective-permute-start(f32[16,1024]{1,0:T(8,128)S(1)} %get-tuple-element.31), channel_id=1, source_target_pairs={{0,64},{16,80},{32,96},{48,112},{64,0},{80,16},{96,32},{112,48},{1... | collective-permute-start | bytes 196616 | tf_op jit(solution)/shard_map/ppermute | solution.py:510
  125.4 2.1 %collective-permute-done.14.in2 = f32[16,1024]{1,0:T(8,128)S(1)} collective-permute-done((f32[16,1024]{1,0:T(8,128)S(1)}, f32[16,1024]{1,0:T(8,128)S(1)}, u32[]{:S(2)}, u32[]{:S(2)}) %collective-permute-start.14) | collective-permute-done | bytes 65568 | tf_op jit(solution)/shard_map/ppermute | solution.py:510
  130.1 3.5 %all-to-all-start.1 = ((f32[16,8,128]{2,1,0:T(8,128)}), f32[16,8,128]{2,1,0:T(8,128)S(1)}, u32[]{:S(2)}, u32[]{:S(2)}) async-start(f32[16,8,128]{2,1,0:T(8,128)} %filter_rows.1), calls=%async_computation.1 | async-start | bytes 131072 | tf_op jit(solution)/shard_map/all_to_all | solution.py:536
  134.6 6.7 %all-to-all-done.1 = f32[16,8,128]{2,1,0:T(8,128)S(1)} async-done(((f32[16,8,128]{2,1,0:T(8,128)}), f32[16,8,128]{2,1,0:T(8,128)S(1)}, u32[]{:S(2)}, u32[]{:S(2)}) %all-to-all-start.1) | async-done | bytes 65568 | tf_op jit(solution)/shard_map/all_to_all | solution.py:536
  (59 shorter events, 28.0 us)
Async XLA Ops:
  25.3 29.8 %collective-permute-start.1 = (s16[3024,128]{1,0:T(8,128)(2,1)S(1)}, s16[3024,128]{1,0:T(8,128)(2,1)S(1)}, u32[]{:S(2)}, u32[]{:S(2)}) collective-permute-start(s16[3024,128]{1,0:T(8,128)(2,1)S(1)} %product_coded.9), channel_id=1, source_target_pairs={{0,8},{1,9},{2,10},{3,11},{4,12},{5,13},{6,14},{7,15},{8,0},{9,1},... | collective-permute-start | bytes 2322440 | tf_op jit(solution)/shard_map/ppermute | solution.py:302
  31.5 31.1 %collective-permute-start = (s16[3024,128]{1,0:T(8,128)(2,1)S(1)}, s16[3024,128]{1,0:T(8,128)(2,1)S(1)}, u32[]{:S(2)}, u32[]{:S(2)}) collective-permute-start(s16[3024,128]{1,0:T(8,128)(2,1)S(1)} %product_coded.8), channel_id=1, source_target_pairs={{0,4},{1,5},{2,6},{3,7},{4,8},{5,9},{6,10},{7,11},{8,12},{9,13},{1... | collective-permute-start | bytes 2322440 | tf_op jit(solution)/shard_map/ppermute | solution.py:302
  35.0 28.0 %collective-permute-start.2 = (s16[3024,128]{1,0:T(8,128)(2,1)S(1)}, s16[3024,128]{1,0:T(8,128)(2,1)S(1)}, u32[]{:S(2)}, u32[]{:S(2)}) collective-permute-start(s16[3024,128]{1,0:T(8,128)(2,1)S(1)} %product_coded.6.after), channel_id=1, source_target_pairs={{0,12},{1,13},{2,14},{3,15},{4,0},{5,1},{6,2},{7,3},{8,4},{9,5},{1... | collective-permute-start | bytes 2322440 | tf_op jit(solution)/shard_map/ppermute | solution.py:302
  45.9 24.2 %collective-permute-start.7 = (s16[1952,128]{1,0:T(8,128)(2,1)S(1)}, s16[1952,128]{1,0:T(8,128)(2,1)S(1)}, u32[]{:S(2)}, u32[]{:S(2)}) collective-permute-start(s16[1952,128]{1,0:T(8,128)(2,1)S(1)} %product_coded.11), channel_id=1, source_target_pairs={{0,2},{1,3},{2,0},{3,1},{4,6},{5,7},{6,4},{7,5},{8,10},{9,11},{10,... | collective-permute-start | bytes 1499144 | tf_op jit(solution)/shard_map/ppermute | solution.py:302
  51.9 20.8 %collective-permute-start.6 = (s16[1952,128]{1,0:T(8,128)(2,1)S(1)}, s16[1952,128]{1,0:T(8,128)(2,1)S(1)}, u32[]{:S(2)}, u32[]{:S(2)}) collective-permute-start(s16[1952,128]{1,0:T(8,128)(2,1)S(1)} %product_coded.10), channel_id=1, source_target_pairs={{0,1},{1,2},{2,3},{3,0},{4,5},{5,6},{6,7},{7,4},{8,9},{9,10},{10,1... | collective-permute-start | bytes 1499144 | tf_op jit(solution)/shard_map/ppermute | solution.py:302
  55.1 18.3 %collective-permute-start.8 = (s16[1952,128]{1,0:T(8,128)(2,1)S(1)}, s16[1952,128]{1,0:T(8,128)(2,1)S(1)}, u32[]{:S(2)}, u32[]{:S(2)}) collective-permute-start(s16[1952,128]{1,0:T(8,128)(2,1)S(1)} %product_coded.7.after), channel_id=1, source_target_pairs={{0,3},{1,0},{2,1},{3,2},{4,7},{5,4},{6,5},{7,6},{8,11},{9,8},{10,9... | collective-permute-start | bytes 1499144 | tf_op jit(solution)/shard_map/ppermute | solution.py:302
  65.1 13.2 %collective-permute-start.3 = (s16[768,128]{1,0:T(8,128)(2,1)S(1)}, s16[768,128]{1,0:T(8,128)(2,1)S(1)}, u32[]{:S(2)}, u32[]{:S(2)}) collective-permute-start(s16[768,128]{1,0:T(8,128)(2,1)S(1)} %get-tuple-element.19), channel_id=1, source_target_pairs={{0,2},{1,3},{2,0},{3,1},{4,6},{5,7},{6,4},{7,5},{8,10},{9,11},{10,... | collective-permute-start | bytes 589832 | tf_op jit(solution)/shard_map/ppermute | solution.py:302
  69.1 10.5 %collective-permute-start.4 = (s16[768,128]{1,0:T(8,128)(2,1)S(1)}, s16[768,128]{1,0:T(8,128)(2,1)S(1)}, u32[]{:S(2)}, u32[]{:S(2)}) collective-permute-start(s16[768,128]{1,0:T(8,128)(2,1)S(1)} %get-tuple-element.20), channel_id=1, source_target_pairs={{0,1},{1,2},{2,3},{3,0},{4,5},{5,6},{6,7},{7,4},{8,9},{9,10},{10,1... | collective-permute-start | bytes 589832 | tf_op jit(solution)/shard_map/ppermute | solution.py:302
  70.1 10.3 %collective-permute-start.5 = (s16[768,128]{1,0:T(8,128)(2,1)S(1)}, s16[768,128]{1,0:T(8,128)(2,1)S(1)}, u32[]{:S(2)}, u32[]{:S(2)}) collective-permute-start(s16[768,128]{1,0:T(8,128)(2,1)S(1)} %get-tuple-element.21), channel_id=1, source_target_pairs={{0,3},{1,0},{2,1},{3,2},{4,7},{5,4},{6,5},{7,6},{8,11},{9,8},{10,9... | collective-permute-start | bytes 589832 | tf_op jit(solution)/shard_map/ppermute | solution.py:302
  75.0 16.1 %collective-permute-start.10 = (s16[496,128]{1,0:T(8,128)(2,1)S(1)}, s16[496,128]{1,0:T(8,128)(2,1)S(1)}, u32[]{:S(2)}, u32[]{:S(2)}) collective-permute-start(s16[496,128]{1,0:T(8,128)(2,1)S(1)} %get-tuple-element.25), channel_id=1, source_target_pairs={{0,4},{1,5},{2,6},{3,7},{4,8},{5,9},{6,10},{7,11},{8,12},{9,13},{1... | collective-permute-start | bytes 380936 | tf_op jit(solution)/shard_map/ppermute | solution.py:302
  75.3 15.8 %collective-permute-start.11 = (s16[496,128]{1,0:T(8,128)(2,1)S(1)}, s16[496,128]{1,0:T(8,128)(2,1)S(1)}, u32[]{:S(2)}, u32[]{:S(2)}) collective-permute-start(s16[496,128]{1,0:T(8,128)(2,1)S(1)} %get-tuple-element.26), channel_id=1, source_target_pairs={{0,12},{1,13},{2,14},{3,15},{4,0},{5,1},{6,2},{7,3},{8,4},{9,5},{1... | collective-permute-start | bytes 380936 | tf_op jit(solution)/shard_map/ppermute | solution.py:302
  78.3 12.8 %collective-permute-start.9 = (s16[496,128]{1,0:T(8,128)(2,1)S(1)}, s16[496,128]{1,0:T(8,128)(2,1)S(1)}, u32[]{:S(2)}, u32[]{:S(2)}) collective-permute-start(s16[496,128]{1,0:T(8,128)(2,1)S(1)} %get-tuple-element.24), channel_id=1, source_target_pairs={{0,8},{1,9},{2,10},{3,11},{4,12},{5,13},{6,14},{7,15},{8,0},{9,1},... | collective-permute-start | bytes 380936 | tf_op jit(solution)/shard_map/ppermute | solution.py:302
  91.1 37.1 %copy-start.1 = (f32[256,256]{1,0:T(8,128)S(1)}, f32[256,256]{1,0:T(8,128)}, u32[]{:S(2)}) copy-start(f32[256,256]{1,0:T(8,128)} %constant.98.clone.second) | copy-start | bytes 786436
  91.1 37.1 %copy-start.2 = (f32[256,256]{1,0:T(8,128)S(1)}, f32[256,256]{1,0:T(8,128)}, u32[]{:S(2)}) copy-start(f32[256,256]{1,0:T(8,128)} %constant.99.clone.third) | copy-start | bytes 786436
  91.2 37.0 %copy-start.3 = (f32[128,256]{1,0:T(8,128)S(1)}, f32[128,256]{1,0:T(8,128)}, u32[]{:S(2)}) copy-start(f32[128,256]{1,0:T(8,128)} %constant.100.clone.last) | copy-start | bytes 393220
  91.2 37.0 %copy-start.4 = (f32[256,128]{1,0:T(8,128)S(1)}, f32[256,128]{1,0:T(8,128)}, u32[]{:S(2)}) copy-start(f32[256,128]{1,0:T(8,128)} %constant.97.clone.first) | copy-start | bytes 393220
  91.2 37.0 %copy-start.5 = (f32[128,128]{1,0:T(8,128)S(1)}, f32[128,128]{1,0:T(8,128)}, u32[]{:S(2)}) copy-start(f32[128,128]{1,0:T(8,128)} %constant.101.clone.tc) | copy-start | bytes 196612
  91.2 37.0 %copy-start.6 = (f32[128,128]{1,0:T(8,128)S(1)}, f32[128,128]{1,0:T(8,128)}, u32[]{:S(2)}) copy-start(f32[128,128]{1,0:T(8,128)} %constant.102.clone.ts) | copy-start | bytes 196612
  100.0 17.3 %all-to-all-start = ((f32[16,8,1152]{2,1,0:T(8,128)}), f32[16,8,1152]{2,1,0:T(8,128)S(1)}, u32[]{:S(2)}, u32[]{:S(2)}) async-start(f32[16,8,1152]{2,1,0:T(8,128)} %get-tuple-element.29), calls=%async_computation | async-start | bytes 1179648 | tf_op jit(solution)/shard_map/all_to_all | solution.py:533
  117.9 1.6 %collective-permute-start.12 = (f32[4,16,1024]{2,1,0:T(8,128)S(1)}, f32[4,16,1024]{2,1,0:T(8,128)S(1)}, u32[]{:S(2)}, u32[]{:S(2)}) collective-permute-start(f32[4,16,1024]{2,1,0:T(8,128)S(1)} %dynamic-slice_bitcast_fusion), channel_id=1, source_target_pairs={{0,16},{16,0},{32,48},{48,32},{64,80},{80,64},{96,112},{112,96},{1... | collective-permute-start | bytes 786440 | tf_op jit(solution)/shard_map/ppermute | solution.py:506
  119.6 5.7 %collective-permute-start.13 = (f32[16,1024]{1,0:T(8,128)S(1)}, f32[16,1024]{1,0:T(8,128)S(1)}, u32[]{:S(2)}, u32[]{:S(2)}) collective-permute-start(f32[16,1024]{1,0:T(8,128)S(1)} %get-tuple-element.32), channel_id=1, source_target_pairs={{0,32},{16,48},{32,64},{48,80},{64,96},{80,112},{96,0},{112,16},{1... | collective-permute-start | bytes 196616 | tf_op jit(solution)/shard_map/ppermute | solution.py:510
  121.2 6.2 %collective-permute-start.14 = (f32[16,1024]{1,0:T(8,128)S(1)}, f32[16,1024]{1,0:T(8,128)S(1)}, u32[]{:S(2)}, u32[]{:S(2)}) collective-permute-start(f32[16,1024]{1,0:T(8,128)S(1)} %get-tuple-element.31), channel_id=1, source_target_pairs={{0,64},{16,80},{32,96},{48,112},{64,0},{80,16},{96,32},{112,48},{1... | collective-permute-start | bytes 196616 | tf_op jit(solution)/shard_map/ppermute | solution.py:510
  123.9 4.3 %collective-permute-start.15 = (f32[16,1024]{1,0:T(8,128)S(1)}, f32[16,1024]{1,0:T(8,128)S(1)}, u32[]{:S(2)}, u32[]{:S(2)}) collective-permute-start(f32[16,1024]{1,0:T(8,128)S(1)} %get-tuple-element.30), channel_id=1, source_target_pairs={{0,96},{16,112},{32,0},{48,16},{64,32},{80,48},{96,64},{112,80},{1... | collective-permute-start | bytes 196616 | tf_op jit(solution)/shard_map/ppermute | solution.py:510
  130.1 11.1 %all-to-all-start.1 = ((f32[16,8,128]{2,1,0:T(8,128)}), f32[16,8,128]{2,1,0:T(8,128)S(1)}, u32[]{:S(2)}, u32[]{:S(2)}) async-start(f32[16,8,128]{2,1,0:T(8,128)} %filter_rows.1), calls=%async_computation.1 | async-start | bytes 131072 | tf_op jit(solution)/shard_map/all_to_all | solution.py:536
  (4 other events, 57.1 us)

commit v3 on v2

--- a/solution.py
+++ b/solution.py
@@ -330,19 +330,20 @@
 
 def collocate_kernel(half, spot, keep, ids, own, in1, in2, in3, cols, rows, after, *rest):
     size = FOLD[half]
-    before = rest[0] if half else None
-    density, out, stacked, right, held, held_cols, sems = rest[half:]
+    if half == 0:
+        density, out, held_cols, stacked, right, held, sems = rest
+    else:
+        before, held_cols, density, out, stacked, right, held, sems = rest
     count = ROWS[half]
     tiles = 16384 // POINTS
 
     def copies(g):
         span = pl.ds(pl.multiple_of(g * POINTS, POINTS), POINTS)
-        return (
-            pltpu.make_async_copy(cols.at[0, :, span], held_cols.at[g], sems.at[0, g]),
-            pltpu.make_async_copy(
-                rows.at[pl.ds(CUT[half] // 8, count // 8), :, span], held.at[g], sems.at[1, g]
-            ),
-        )
+        planes = rows.at[pl.ds(CUT[half] // 8, count // 8), :, span]
+        fetched = [pltpu.make_async_copy(planes, held.at[g], sems.at[1, g])]
+        if half == 0:
+            fetched.append(pltpu.make_async_copy(cols.at[0, :, span], held_cols.at[g], sems.at[0, g]))
+        return fetched
 
     for g in range(tiles):
         for copy in copies(g):
@@ -416,19 +417,19 @@
         + [vmem] * 4
         + [pl.BlockSpec(memory_space=pltpu.HBM)] * 2
         + [pl.BlockSpec(memory_space=pl.ANY)]
-        + [vmem] * half,
-        out_specs=[vmem] * 2,
+        + [vmem] * (2 * half),
+        out_specs=[vmem] * (3 - half),
         scratch_shapes=[
             pltpu.VMEM((count, 256), BF16),
             pltpu.VMEM((256, POINTS), BF16),
             pltpu.VMEM((tiles, count // 8, 8, POINTS), BF16),
-            pltpu.VMEM((tiles, BS, POINTS), BF16),
             pltpu.SemaphoreType.DMA((2, tiles)),
         ],
         out_shape=[
             jax.ShapeDtypeStruct((count // 8, 8, BS), BF16),
             jax.ShapeDtypeStruct((16, 8, wide), F32),
-        ],
+        ]
+        + [pltpu.VMEM((tiles, BS, POINTS), BF16)] * (1 - half),
         compiler_params=pltpu.CompilerParams(vmem_limit_bytes=(38, 28)[half] * MIB),
         cost_estimate=pl.CostEstimate(flops=1000, bytes_accessed=1000, transcendentals=0),
         name="collocate",
@@ -524,11 +525,11 @@
         after = sums[half][0]
     for half in range(2):
         own, parts = sums[half]
-        density, after = collocate(
+        density, after, *held = collocate(
             half, spot, keep, ids, own, parts, basis_cols, by_point, before, after
         )
         densities.append(density)
-        before = [after]
+        before = [after] + held
     points = after
     points = lax.all_to_all(points, "col", split_axis=0, concat_axis=0, tiled=True)
     pieces = scatter_rows(sum_bricks(points))

time: 142 us -> 142 us (level)
  no operation moved by 1% of the time
where the time goes in v3:
time: 142 us; the launch traced here: 141 us
  Pallas kernels  70.5 us (50%)
  starting transfers between devices  41.2 us (29%)
  waiting for transfers between devices  25.6 us (18%)
  local copies, waits for them, and re-layouts  1.95 us (1%)
    ppermute x12, starting transfers between devices, send(): return lax.ppermute(array, 'col', turn(d, 0) if axis == 0 else turn(0, d))  25.2 us
    pallas_call x2, Pallas kernels, collocate(): pl.pallas_call(functools.partial(collocate_kernel, half), in_specs=[pl.Bl...  18.9 us
    pallas_call x8, Pallas kernels, product_group(): pl.pallas_call(functools.partial(product_kernel, half, d), in_specs=[pl.B...  18.6 us
    pallas_call x1, Pallas kernels, pack_right(): pl.pallas_call(pack_right_kernel, grid=(8,), in_specs=[pl.BlockSpec((2, B...  12.5 us
    pallas_call x2, Pallas kernels, pack_left(): pl.pallas_call(functools.partial(pack_left_kernel, count // 2), grid=(ROW...  12 us
    all_to_all x1, waiting for transfers between devices, shards(): lax.all_to_all(points, 'col', split_axis=0, concat_axis=0, tiled=True)  10.7 us
    all_to_all x1, waiting for transfers between devices, shards(): lax.all_to_all(filtered, 'col', split_axis=0, concat_axis=0, tiled=True)  6.71 us
    all_to_all x1, starting transfers between devices, shards(): lax.all_to_all(points, 'col', split_axis=0, concat_axis=0, tiled=True)  6.61 us
  transfers between devices with their start and end apart: 18, of which 11 were waited for; matrix products, arithmetic and copies ran while one was open for 1% of the time, Pallas kernels for 26%

profile of v3, /device:TPU:0, one launch (start us, length us, event | category | flops | bytes accessed | tf_op | source)
XLA Modules:
  0.0 141.3 jit_solution(16915879127920973261)
XLA Ops:
  1.9 12.5 %pack_right.1 = (bf16[16,2304,128]{2,1,0:T(8,128)(2,1)S(1)}, bf16[2304,256]{1,0:T(8,128)(2,1)S(1)}) custom-call(bf16[16,138,16,138]{3,2,1,0:T(8,128)(2,1)} %bitcast.39, s32[2]{0:T(128)S(1)} %pad_add_fusion.others_0_.spot.place, f32[128,128]{1,0:T(8,128)S(1)} %bitcast.29), custom_call_target="tpu_custom_call" | custom-call | flops 1000 | bytes 1000 | tf_op jit(solution)/shard_map/pack_right/pallas_call | solution.py:121
  14.5 7.0 %pack_left.2.left = bf16[672,2304]{1,0:T(8,128)(2,1)S(1)} custom-call(s32[8,16]{1,0:T(8,128)S(1)} %copy-done.7, bf16[8,138,16,138]{3,2,1,0:T(8,128)(2,1)} %bitcast.37, bf16[16,2304,128]{2,1,0:T(8,128)(2,1)S(1)} %get-tuple-element.17.after.near), custom_call_target="tpu_custom_call" | custom-call | flops 1000 | bytes 1000 | tf_op jit(solution)/shard_map/pack_left/pallas_call | solution.py:75
  22.5 2.8 %product_coded.9 = s16[3024,128]{1,0:T(8,128)(2,1)S(1)} custom-call(s32[2]{0:T(128)S(1)} %pad_add_fusion.others_0_.spot.place, bf16[672,2304]{1,0:T(8,128)(2,1)S(1)} %pack_left.2.left, bf16[16,2304,128]{2,1,0:T(8,128)(2,1)S(1)} %get-tuple-element.17.after.near, f32[672,256]{1,0:T(8,128)S(1)} %product_tails.2.tails.after, f32[672,256]{1,0:T(8,128)S(1)} %product_tails.2.tails.after), custom_call_target="tpu_custom_call" | custom-call | flops 1000 | bytes 1000 | tf_op jit(solution)/shard_map/product_coded/pallas_call | solution.py:235
  25.3 3.4 %collective-permute-start.1 = (s16[3024,128]{1,0:T(8,128)(2,1)S(1)}, s16[3024,128]{1,0:T(8,128)(2,1)S(1)}, u32[]{:S(2)}, u32[]{:S(2)}) collective-permute-start(s16[3024,128]{1,0:T(8,128)(2,1)S(1)} %product_coded.9), channel_id=1, source_target_pairs={{0,8},{1,9},{2,10},{3,11},{4,12},{5,13},{6,14},{7,15},{8,0},{9,1},... | collective-permute-start | bytes 2322440 | tf_op jit(solution)/shard_map/ppermute | solution.py:302
  28.7 2.8 %product_coded.8 = s16[3024,128]{1,0:T(8,128)(2,1)S(1)} custom-call(s32[2]{0:T(128)S(1)} %pad_add_fusion.others_0_.spot.place, bf16[672,2304]{1,0:T(8,128)(2,1)S(1)} %pack_left.2.left, bf16[16,2304,128]{2,1,0:T(8,128)(2,1)S(1)} %get-tuple-element.17.after.near, f32[672,256]{1,0:T(8,128)S(1)} %product_tails.2.tails.after, f32[672,256]{1,0:T(8,128)S(1)} %product_tails.2.tails.after), custom_call_target="tpu_custom_call" | custom-call | flops 1000 | bytes 1000 | tf_op jit(solution)/shard_map/product_coded/pallas_call | solution.py:235
  32.2 2.8 %product_coded.6.after = s16[3024,128]{1,0:T(8,128)(2,1)S(1)} custom-call(s32[2]{0:T(128)S(1)} %pad_add_fusion.others_0_.spot.place, bf16[672,2304]{1,0:T(8,128)(2,1)S(1)} %pack_left.2.left, bf16[16,2304,128]{2,1,0:T(8,128)(2,1)S(1)} %get-tuple-element.17.after.near, f32[672,256]{1,0:T(8,128)S(1)} %product_tails.2.tails.after, ...), custom_call_target="tpu_custom_call" | custom-call | flops 1000 | bytes 1000 | tf_op jit(solution)/shard_map/product_coded/pallas_call | solution.py:235
  35.0 2.6 %collective-permute-start.2 = (s16[3024,128]{1,0:T(8,128)(2,1)S(1)}, s16[3024,128]{1,0:T(8,128)(2,1)S(1)}, u32[]{:S(2)}, u32[]{:S(2)}) collective-permute-start(s16[3024,128]{1,0:T(8,128)(2,1)S(1)} %product_coded.6.after), channel_id=1, source_target_pairs={{0,12},{1,13},{2,14},{3,15},{4,0},{5,1},{6,2},{7,3},{8,4},{9,5},{1... | collective-permute-start | bytes 2322440 | tf_op jit(solution)/shard_map/ppermute | solution.py:302
  37.6 5.0 %pack_left.3.left = bf16[432,2304]{1,0:T(8,128)(2,1)S(1)} custom-call(s32[8,16]{1,0:T(8,128)S(1)} %copy-done.7, bf16[8,138,16,138]{3,2,1,0:T(8,128)(2,1)} %bitcast.38, s16[3024,128]{1,0:T(8,128)(2,1)S(1)} %product_coded.6.after), custom_call_target="tpu_custom_call" | custom-call | flops 1000 | bytes 1000 | tf_op jit(solution)/shard_map/pack_left/pallas_call | solution.py:75
  43.8 2.1 %product_coded.11 = s16[1952,128]{1,0:T(8,128)(2,1)S(1)} custom-call(s32[2]{0:T(128)S(1)} %pad_add_fusion.others_0_.spot.place, bf16[432,2304]{1,0:T(8,128)(2,1)S(1)} %pack_left.3.left, bf16[16,2304,128]{2,1,0:T(8,128)(2,1)S(1)} %get-tuple-element.17.after.near, f32[432,256]{1,0:T(8,128)S(1)} %product_tails.3.tails.after, ...), custom_call_target="tpu_custom_call" | custom-call | flops 1000 | bytes 1000 | tf_op jit(solution)/shard_map/product_coded/pallas_call | solution.py:235
  45.9 4.0 %collective-permute-start.7 = (s16[1952,128]{1,0:T(8,128)(2,1)S(1)}, s16[1952,128]{1,0:T(8,128)(2,1)S(1)}, u32[]{:S(2)}, u32[]{:S(2)}) collective-permute-start(s16[1952,128]{1,0:T(8,128)(2,1)S(1)} %product_coded.11), channel_id=1, source_target_pairs={{0,2},{1,3},{2,0},{3,1},{4,6},{5,7},{6,4},{7,5},{8,10},{9,11},{10,... | collective-permute-start | bytes 1499144 | tf_op jit(solution)/shard_map/ppermute | solution.py:302
  55.1 2.5 %collective-permute-start.8 = (s16[1952,128]{1,0:T(8,128)(2,1)S(1)}, s16[1952,128]{1,0:T(8,128)(2,1)S(1)}, u32[]{:S(2)}, u32[]{:S(2)}) collective-permute-start(s16[1952,128]{1,0:T(8,128)(2,1)S(1)} %product_coded.7.after), channel_id=1, source_target_pairs={{0,3},{1,0},{2,1},{3,2},{4,7},{5,4},{6,5},{7,6},{8,11},{9,8},{10,9... | collective-permute-start | bytes 1499144 | tf_op jit(solution)/shard_map/ppermute | solution.py:302
  57.6 2.3 %product_own.2.after.own = f32[3024,128]{1,0:T(8,128)S(1)} custom-call(s32[2]{0:T(128)S(1)} %pad_add_fusion.others_0_.spot.place, bf16[672,2304]{1,0:T(8,128)(2,1)S(1)} %pack_left.2.left, bf16[16,2304,128]{2,1,0:T(8,128)(2,1)S(1)} %get-tuple-element.17.after.near, f32[672,256]{1,0:T(8,128)S(1)} %product_tails.2.tails.after, ...), custom_call_target="tpu_custom_call" | custom-call | flops 1000 | bytes 1000 | tf_op jit(solution)/shard_map/product_own/pallas_call | solution.py:235
  63.0 2.1 %merge.2 = (f32[768,128]{1,0:T(8,128)S(1)}, s16[768,128]{1,0:T(8,128)(2,1)S(1)}, s16[768,128]{1,0:T(8,128)(2,1)S(1)}, s16[768,128]{1,0:T(8,128)(2,1)S(1)}) custom-call(s32[2]{0:T(128)S(1)} %pad_add_fusion.others_0_.spot.place, f32[3024,128]{1,0:T(8,128)S(1)} %product_own.2.after.own, s16[3024,128]{1,0:T(8,128)(2,1)S(1)} %collective-permute-done.in1, ...), custom_call_target="tpu_custom_call" | custom-call | flops 1000 | bytes 1000 | tf_op jit(solution)/shard_map/merge/pallas_call | solution.py:285
  65.1 3.9 %collective-permute-start.3 = (s16[768,128]{1,0:T(8,128)(2,1)S(1)}, s16[768,128]{1,0:T(8,128)(2,1)S(1)}, u32[]{:S(2)}, u32[]{:S(2)}) collective-permute-start(s16[768,128]{1,0:T(8,128)(2,1)S(1)} %get-tuple-element.20), channel_id=1, source_target_pairs={{0,2},{1,3},{2,0},{3,1},{4,6},{5,7},{6,4},{7,5},{8,10},{9,11},{10,... | collective-permute-start | bytes 589832 | tf_op jit(solution)/shard_map/ppermute | solution.py:302
  70.1 2.2 %collective-permute-start.5 = (s16[768,128]{1,0:T(8,128)(2,1)S(1)}, s16[768,128]{1,0:T(8,128)(2,1)S(1)}, u32[]{:S(2)}, u32[]{:S(2)}) collective-permute-start(s16[768,128]{1,0:T(8,128)(2,1)S(1)} %get-tuple-element.22), channel_id=1, source_target_pairs={{0,3},{1,0},{2,1},{3,2},{4,7},{5,4},{6,5},{7,6},{8,11},{9,8},{10,9... | collective-permute-start | bytes 589832 | tf_op jit(solution)/shard_map/ppermute | solution.py:302
  75.3 3.0 %collective-permute-start.11 = (s16[496,128]{1,0:T(8,128)(2,1)S(1)}, s16[496,128]{1,0:T(8,128)(2,1)S(1)}, u32[]{:S(2)}, u32[]{:S(2)}) collective-permute-start(s16[496,128]{1,0:T(8,128)(2,1)S(1)} %get-tuple-element.27), channel_id=1, source_target_pairs={{0,12},{1,13},{2,14},{3,15},{4,0},{5,1},{6,2},{7,3},{8,4},{9,5},{1... | collective-permute-start | bytes 380936 | tf_op jit(solution)/shard_map/ppermute | solution.py:302
  80.4 10.6 %collocate.2 = (bf16[84,8,138]{2,1,0:T(8,128)(2,1)S(1)}, f32[16,8,1024]{2,1,0:T(8,128)S(1)}, bf16[8,138,2048]{2,1,0:T(8,128)(2,1)S(1)}) custom-call(s32[2]{0:T(128)S(1)} %pad_add_fusion.others_0_.spot.place, s32[8]{0:T(128)S(1)} %bitcast.31, s32[8]{0:T(128)S(1)} %bitcast.33, f32[768,128]{1,0:T(8,128)S(1)} %get-tuple-element.19.after.own, ...), custom_call_target="tpu_custom_call" | custom-call | flops 1000 | bytes 1000 | tf_op jit(solution)/shard_map/collocate/pallas_call | solution.py:414
  91.1 8.4 %collocate.3 = (bf16[54,8,138]{2,1,0:T(8,128)(2,1)S(1)}, f32[16,8,1152]{2,1,0:T(8,128)}) custom-call(s32[2]{0:T(128)S(1)} %pad_add_fusion.others_0_.spot.place, s32[8]{0:T(128)S(1)} %bitcast.32, s32[8]{0:T(128)S(1)} %bitcast.34, f32[496,128]{1,0:T(8,128)S(1)} %get-tuple-element.23.after.own, s16[496,128]{1,0:T(8,128)(2,1)S(1)} %collective-permute-done.9.in1, ...), custom_call_target="tpu_custom_call" | custom-call | flops 1000 | bytes 1000 | tf_op jit(solution)/shard_map/collocate/pallas_call | solution.py:414
  99.4 6.6 %all-to-all-start = ((f32[16,8,1152]{2,1,0:T(8,128)}), f32[16,8,1152]{2,1,0:T(8,128)S(1)}, u32[]{:S(2)}, u32[]{:S(2)}) async-start(f32[16,8,1152]{2,1,0:T(8,128)} %get-tuple-element.31), calls=%async_computation | async-start | bytes 1179648 | tf_op jit(solution)/shard_map/all_to_all | solution.py:534
  106.1 10.7 %all-to-all-done.points = f32[16,8,1152]{2,1,0:T(8,128)S(1)} async-done(((f32[16,8,1152]{2,1,0:T(8,128)}), f32[16,8,1152]{2,1,0:T(8,128)S(1)}, u32[]{:S(2)}, u32[]{:S(2)}) %all-to-all-start) | async-done | bytes 589856 | tf_op jit(solution)/shard_map/all_to_all | solution.py:534
  120.6 2.7 %collective-permute-start.14 = (f32[16,1024]{1,0:T(8,128)S(1)}, f32[16,1024]{1,0:T(8,128)S(1)}, u32[]{:S(2)}, u32[]{:S(2)}) collective-permute-start(f32[16,1024]{1,0:T(8,128)S(1)} %get-tuple-element.33), channel_id=1, source_target_pairs={{0,64},{16,80},{32,96},{48,112},{64,0},{80,16},{96,32},{112,48},{1... | collective-permute-start | bytes 196616 | tf_op jit(solution)/shard_map/ppermute | solution.py:511
  124.8 2.1 %collective-permute-done.14.in2 = f32[16,1024]{1,0:T(8,128)S(1)} collective-permute-done((f32[16,1024]{1,0:T(8,128)S(1)}, f32[16,1024]{1,0:T(8,128)S(1)}, u32[]{:S(2)}, u32[]{:S(2)}) %collective-permute-start.14) | collective-permute-done | bytes 65568 | tf_op jit(solution)/shard_map/ppermute | solution.py:511
  129.6 3.5 %all-to-all-start.1 = ((f32[16,8,128]{2,1,0:T(8,128)}), f32[16,8,128]{2,1,0:T(8,128)S(1)}, u32[]{:S(2)}, u32[]{:S(2)}) async-start(f32[16,8,128]{2,1,0:T(8,128)} %filter_rows.1), calls=%async_computation.1 | async-start | bytes 131072 | tf_op jit(solution)/shard_map/all_to_all | solution.py:537
  134.0 6.7 %all-to-all-done.1 = f32[16,8,128]{2,1,0:T(8,128)S(1)} async-done(((f32[16,8,128]{2,1,0:T(8,128)}), f32[16,8,128]{2,1,0:T(8,128)S(1)}, u32[]{:S(2)}, u32[]{:S(2)}) %all-to-all-start.1) | async-done | bytes 65568 | tf_op jit(solution)/shard_map/all_to_all | solution.py:537
  (59 shorter events, 28.0 us)
Async XLA Ops:
  25.3 29.8 %collective-permute-start.1 = (s16[3024,128]{1,0:T(8,128)(2,1)S(1)}, s16[3024,128]{1,0:T(8,128)(2,1)S(1)}, u32[]{:S(2)}, u32[]{:S(2)}) collective-permute-start(s16[3024,128]{1,0:T(8,128)(2,1)S(1)} %product_coded.9), channel_id=1, source_target_pairs={{0,8},{1,9},{2,10},{3,11},{4,12},{5,13},{6,14},{7,15},{8,0},{9,1},... | collective-permute-start | bytes 2322440 | tf_op jit(solution)/shard_map/ppermute | solution.py:302
  31.5 31.1 %collective-permute-start = (s16[3024,128]{1,0:T(8,128)(2,1)S(1)}, s16[3024,128]{1,0:T(8,128)(2,1)S(1)}, u32[]{:S(2)}, u32[]{:S(2)}) collective-permute-start(s16[3024,128]{1,0:T(8,128)(2,1)S(1)} %product_coded.8), channel_id=1, source_target_pairs={{0,4},{1,5},{2,6},{3,7},{4,8},{5,9},{6,10},{7,11},{8,12},{9,13},{1... | collective-permute-start | bytes 2322440 | tf_op jit(solution)/shard_map/ppermute | solution.py:302
  35.0 28.0 %collective-permute-start.2 = (s16[3024,128]{1,0:T(8,128)(2,1)S(1)}, s16[3024,128]{1,0:T(8,128)(2,1)S(1)}, u32[]{:S(2)}, u32[]{:S(2)}) collective-permute-start(s16[3024,128]{1,0:T(8,128)(2,1)S(1)} %product_coded.6.after), channel_id=1, source_target_pairs={{0,12},{1,13},{2,14},{3,15},{4,0},{5,1},{6,2},{7,3},{8,4},{9,5},{1... | collective-permute-start | bytes 2322440 | tf_op jit(solution)/shard_map/ppermute | solution.py:302
  45.9 24.2 %collective-permute-start.7 = (s16[1952,128]{1,0:T(8,128)(2,1)S(1)}, s16[1952,128]{1,0:T(8,128)(2,1)S(1)}, u32[]{:S(2)}, u32[]{:S(2)}) collective-permute-start(s16[1952,128]{1,0:T(8,128)(2,1)S(1)} %product_coded.11), channel_id=1, source_target_pairs={{0,2},{1,3},{2,0},{3,1},{4,6},{5,7},{6,4},{7,5},{8,10},{9,11},{10,... | collective-permute-start | bytes 1499144 | tf_op jit(solution)/shard_map/ppermute | solution.py:302
  51.9 20.8 %collective-permute-start.6 = (s16[1952,128]{1,0:T(8,128)(2,1)S(1)}, s16[1952,128]{1,0:T(8,128)(2,1)S(1)}, u32[]{:S(2)}, u32[]{:S(2)}) collective-permute-start(s16[1952,128]{1,0:T(8,128)(2,1)S(1)} %product_coded.10), channel_id=1, source_target_pairs={{0,1},{1,2},{2,3},{3,0},{4,5},{5,6},{6,7},{7,4},{8,9},{9,10},{10,1... | collective-permute-start | bytes 1499144 | tf_op jit(solution)/shard_map/ppermute | solution.py:302
  55.1 18.3 %collective-permute-start.8 = (s16[1952,128]{1,0:T(8,128)(2,1)S(1)}, s16[1952,128]{1,0:T(8,128)(2,1)S(1)}, u32[]{:S(2)}, u32[]{:S(2)}) collective-permute-start(s16[1952,128]{1,0:T(8,128)(2,1)S(1)} %product_coded.7.after), channel_id=1, source_target_pairs={{0,3},{1,0},{2,1},{3,2},{4,7},{5,4},{6,5},{7,6},{8,11},{9,8},{10,9... | collective-permute-start | bytes 1499144 | tf_op jit(solution)/shard_map/ppermute | solution.py:302
  65.1 13.2 %collective-permute-start.3 = (s16[768,128]{1,0:T(8,128)(2,1)S(1)}, s16[768,128]{1,0:T(8,128)(2,1)S(1)}, u32[]{:S(2)}, u32[]{:S(2)}) collective-permute-start(s16[768,128]{1,0:T(8,128)(2,1)S(1)} %get-tuple-element.20), channel_id=1, source_target_pairs={{0,2},{1,3},{2,0},{3,1},{4,6},{5,7},{6,4},{7,5},{8,10},{9,11},{10,... | collective-permute-start | bytes 589832 | tf_op jit(solution)/shard_map/ppermute | solution.py:302
  69.1 10.5 %collective-permute-start.4 = (s16[768,128]{1,0:T(8,128)(2,1)S(1)}, s16[768,128]{1,0:T(8,128)(2,1)S(1)}, u32[]{:S(2)}, u32[]{:S(2)}) collective-permute-start(s16[768,128]{1,0:T(8,128)(2,1)S(1)} %get-tuple-element.21), channel_id=1, source_target_pairs={{0,1},{1,2},{2,3},{3,0},{4,5},{5,6},{6,7},{7,4},{8,9},{9,10},{10,1... | collective-permute-start | bytes 589832 | tf_op jit(solution)/shard_map/ppermute | solution.py:302
  70.1 10.3 %collective-permute-start.5 = (s16[768,128]{1,0:T(8,128)(2,1)S(1)}, s16[768,128]{1,0:T(8,128)(2,1)S(1)}, u32[]{:S(2)}, u32[]{:S(2)}) collective-permute-start(s16[768,128]{1,0:T(8,128)(2,1)S(1)} %get-tuple-element.22), channel_id=1, source_target_pairs={{0,3},{1,0},{2,1},{3,2},{4,7},{5,4},{6,5},{7,6},{8,11},{9,8},{10,9... | collective-permute-start | bytes 589832 | tf_op jit(solution)/shard_map/ppermute | solution.py:302
  75.0 16.0 %collective-permute-start.10 = (s16[496,128]{1,0:T(8,128)(2,1)S(1)}, s16[496,128]{1,0:T(8,128)(2,1)S(1)}, u32[]{:S(2)}, u32[]{:S(2)}) collective-permute-start(s16[496,128]{1,0:T(8,128)(2,1)S(1)} %get-tuple-element.26), channel_id=1, source_target_pairs={{0,4},{1,5},{2,6},{3,7},{4,8},{5,9},{6,10},{7,11},{8,12},{9,13},{1... | collective-permute-start | bytes 380936 | tf_op jit(solution)/shard_map/ppermute | solution.py:302
  75.3 15.7 %collective-permute-start.11 = (s16[496,128]{1,0:T(8,128)(2,1)S(1)}, s16[496,128]{1,0:T(8,128)(2,1)S(1)}, u32[]{:S(2)}, u32[]{:S(2)}) collective-permute-start(s16[496,128]{1,0:T(8,128)(2,1)S(1)} %get-tuple-element.27), channel_id=1, source_target_pairs={{0,12},{1,13},{2,14},{3,15},{4,0},{5,1},{6,2},{7,3},{8,4},{9,5},{1... | collective-permute-start | bytes 380936 | tf_op jit(solution)/shard_map/ppermute | solution.py:302
  78.3 12.7 %collective-permute-start.9 = (s16[496,128]{1,0:T(8,128)(2,1)S(1)}, s16[496,128]{1,0:T(8,128)(2,1)S(1)}, u32[]{:S(2)}, u32[]{:S(2)}) collective-permute-start(s16[496,128]{1,0:T(8,128)(2,1)S(1)} %get-tuple-element.25), channel_id=1, source_target_pairs={{0,8},{1,9},{2,10},{3,11},{4,12},{5,13},{6,14},{7,15},{8,0},{9,1},... | collective-permute-start | bytes 380936 | tf_op jit(solution)/shard_map/ppermute | solution.py:302
  91.0 36.6 %copy-start.1 = (f32[256,256]{1,0:T(8,128)S(1)}, f32[256,256]{1,0:T(8,128)}, u32[]{:S(2)}) copy-start(f32[256,256]{1,0:T(8,128)} %constant.98.clone.second) | copy-start | bytes 786436
  91.0 36.6 %copy-start.2 = (f32[256,256]{1,0:T(8,128)S(1)}, f32[256,256]{1,0:T(8,128)}, u32[]{:S(2)}) copy-start(f32[256,256]{1,0:T(8,128)} %constant.99.clone.third) | copy-start | bytes 786436
  91.0 36.6 %copy-start.3 = (f32[128,256]{1,0:T(8,128)S(1)}, f32[128,256]{1,0:T(8,128)}, u32[]{:S(2)}) copy-start(f32[128,256]{1,0:T(8,128)} %constant.100.clone.last) | copy-start | bytes 393220
  91.0 36.6 %copy-start.4 = (f32[256,128]{1,0:T(8,128)S(1)}, f32[256,128]{1,0:T(8,128)}, u32[]{:S(2)}) copy-start(f32[256,128]{1,0:T(8,128)} %constant.97.clone.first) | copy-start | bytes 393220
  91.1 36.6 %copy-start.5 = (f32[128,128]{1,0:T(8,128)S(1)}, f32[128,128]{1,0:T(8,128)}, u32[]{:S(2)}) copy-start(f32[128,128]{1,0:T(8,128)} %constant.101.clone.tc) | copy-start | bytes 196612
  91.1 36.6 %copy-start.6 = (f32[128,128]{1,0:T(8,128)S(1)}, f32[128,128]{1,0:T(8,128)}, u32[]{:S(2)}) copy-start(f32[128,128]{1,0:T(8,128)} %constant.102.clone.ts) | copy-start | bytes 196612
  99.4 17.3 %all-to-all-start = ((f32[16,8,1152]{2,1,0:T(8,128)}), f32[16,8,1152]{2,1,0:T(8,128)S(1)}, u32[]{:S(2)}, u32[]{:S(2)}) async-start(f32[16,8,1152]{2,1,0:T(8,128)} %get-tuple-element.31), calls=%async_computation | async-start | bytes 1179648 | tf_op jit(solution)/shard_map/all_to_all | solution.py:534
  117.4 1.6 %collective-permute-start.12 = (f32[4,16,1024]{2,1,0:T(8,128)S(1)}, f32[4,16,1024]{2,1,0:T(8,128)S(1)}, u32[]{:S(2)}, u32[]{:S(2)}) collective-permute-start(f32[4,16,1024]{2,1,0:T(8,128)S(1)} %dynamic-slice_bitcast_fusion), channel_id=1, source_target_pairs={{0,16},{16,0},{32,48},{48,32},{64,80},{80,64},{96,112},{112,96},{1... | collective-permute-start | bytes 786440 | tf_op jit(solution)/shard_map/ppermute | solution.py:507
  119.1 5.7 %collective-permute-start.13 = (f32[16,1024]{1,0:T(8,128)S(1)}, f32[16,1024]{1,0:T(8,128)S(1)}, u32[]{:S(2)}, u32[]{:S(2)}) collective-permute-start(f32[16,1024]{1,0:T(8,128)S(1)} %get-tuple-element.34), channel_id=1, source_target_pairs={{0,32},{16,48},{32,64},{48,80},{64,96},{80,112},{96,0},{112,16},{1... | collective-permute-start | bytes 196616 | tf_op jit(solution)/shard_map/ppermute | solution.py:511
  120.6 6.2 %collective-permute-start.14 = (f32[16,1024]{1,0:T(8,128)S(1)}, f32[16,1024]{1,0:T(8,128)S(1)}, u32[]{:S(2)}, u32[]{:S(2)}) collective-permute-start(f32[16,1024]{1,0:T(8,128)S(1)} %get-tuple-element.33), channel_id=1, source_target_pairs={{0,64},{16,80},{32,96},{48,112},{64,0},{80,16},{96,32},{112,48},{1... | collective-permute-start | bytes 196616 | tf_op jit(solution)/shard_map/ppermute | solution.py:511
  123.4 4.3 %collective-permute-start.15 = (f32[16,1024]{1,0:T(8,128)S(1)}, f32[16,1024]{1,0:T(8,128)S(1)}, u32[]{:S(2)}, u32[]{:S(2)}) collective-permute-start(f32[16,1024]{1,0:T(8,128)S(1)} %get-tuple-element.32), channel_id=1, source_target_pairs={{0,96},{16,112},{32,0},{48,16},{64,32},{80,48},{96,64},{112,80},{1... | collective-permute-start | bytes 196616 | tf_op jit(solution)/shard_map/ppermute | solution.py:511
  129.6 11.1 %all-to-all-start.1 = ((f32[16,8,128]{2,1,0:T(8,128)}), f32[16,8,128]{2,1,0:T(8,128)S(1)}, u32[]{:S(2)}, u32[]{:S(2)}) async-start(f32[16,8,128]{2,1,0:T(8,128)} %filter_rows.1), calls=%async_computation.1 | async-start | bytes 131072 | tf_op jit(solution)/shard_map/all_to_all | solution.py:537
  (4 other events, 57.1 us)
